TPU v7x, 256 devices: a whole 4x4x8 slice. The times are simulated.
256 devices in a mesh: seq: 32 (over z_lo, x, core), head: 8 (over z_hi, y).
Axes of the slice: x: 4, y: 4, z: 8 (z_hi: 2, z_lo: 4; z = z_hi * 4 + z_lo), core: 2. Of those that a mesh axis runs over, the one named last changes fastest.
Arguments:
- queries: bfloat16 [6144, 3072], P(('seq', 'head')), may hold values from -9 to 9
- keys: bfloat16 [6144, 3072], P(('seq', 'head')), may hold values from -9 to 9
- values: bfloat16 [6144, 3072], P(('seq', 'head')), may hold values from -6 to 6
- d_out: bfloat16 [6144, 3072], P(('seq', 'head')), may hold values from -6 to 6
- gain: float32 [16, 3072], replicated, may hold values from 0.3 to 3
- segment_lengths: int32 [8], replicated, may hold values from 672 to 864, as said below
- segment_step: int32 [8], replicated, may hold values from 0 to 15
- block_slot: int32 [32], replicated, may hold values from 0 to 31, each once
Outputs:
- d_queries: bfloat16 [6144, 3072], P(('seq', 'head'))
- d_keys: bfloat16 [6144, 3072], P(('seq', 'head'))
- d_values: bfloat16 [6144, 3072], P(('seq', 'head'))
Inputs may be any that keep to these rules, and one draw needn't show every extreme that they name: `segment_lengths`: the lengths sum to 6144; the longest is exactly 864. `block_slot`: every block position appears once.
All inputs are finite; a program needn't handle non-finite values.
Results may differ from a plain program's by a relative error of at most 0.0071.
Values may be sent and summed in bfloat16 or wider, within the bound.
No kernel may reach another device: no remote copies, remote signals or barrier semaphores. Data moves between devices by JAX's collectives and lax.ppermute only.
A program may use at most 128 MiB of HBM per device.

v0:
```python
import math

import jax
import jax.numpy as jnp
from jax import lax
from jax.sharding import PartitionSpec as P

HD = 128


NEGATIVE = -1e30


def segment_ids(positions, lengths):
    bounds = jnp.cumsum(lengths)
    return jnp.sum((bounds[None, :] <= positions[:, None]).astype(jnp.int32), axis=1)


def slot_lookup(owners, block_slot):
    devices = jnp.arange(block_slot.shape[0], dtype=jnp.int32)
    picked = jnp.where(owners[:, None] == devices[None, :], block_slot[None, :], 0)
    return jnp.sum(picked, axis=1)


def pair_terms(query_rows, cotan_rows, key_rows, value_rows, query_segs, key_segs, scaling):
    scores = (
        jnp.einsum("qhd,khd->hqk", query_rows, key_rows, preferred_element_type=jnp.float32)
        * scaling
    )
    visible = (key_segs[None, :] <= query_segs[:, None])[None]
    scores = jnp.where(visible, scores, NEGATIVE)
    d_probs = jnp.einsum("qhd,khd->hqk", cotan_rows, value_rows, preferred_element_type=jnp.float32)
    return (scores, d_probs, visible)


def partial_stats(scores, d_probs, visible):
    row_max = jnp.max(scores, axis=2)
    weights = jnp.where(visible, jnp.exp(scores - row_max[..., None]), 0.0)
    return (row_max, jnp.sum(weights, axis=2), jnp.sum(weights * d_probs, axis=2))


def combine_stats(first, second):
    row_max = jnp.maximum(first[0], second[0])
    first_factor = jnp.exp(first[0] - row_max)
    second_factor = jnp.exp(second[0] - row_max)
    return (
        row_max,
        first[1] * first_factor + second[1] * second_factor,
        first[2] * first_factor + second[2] * second_factor,
    )


def grad_terms(scores, d_probs, visible, log_total, delta):
    probs = jnp.where(visible, jnp.exp(scores - log_total[..., None]), 0.0)
    shifted = (probs * (d_probs - delta[..., None])).astype(jnp.bfloat16)
    return (probs.astype(jnp.bfloat16), shifted)


def shards(queries, keys, values, d_out, gain, segment_lengths, segment_step, block_slot):
    seq_count = lax.axis_size("seq")
    head_count = lax.axis_size("head")
    sub_rows = queries.shape[0]
    width = queries.shape[1]
    block_rows = sub_rows * head_count
    total_rows = block_rows * seq_count
    head_width = width // head_count
    local_heads = head_width // HD
    scaling = 1.0 / math.sqrt(HD)
    seq_index = lax.axis_index("seq")
    head_index = lax.axis_index("head")
    my_slot = slot_lookup(jnp.reshape(seq_index, (1,)), block_slot)[0]
    token_pos = my_slot * block_rows + head_index * sub_rows + jnp.arange(sub_rows, dtype=jnp.int32)
    token_segs = segment_ids(token_pos, segment_lengths)
    seg_range = jnp.arange(segment_step.shape[0], dtype=jnp.int32)
    seg_steps = jnp.sum(
        jnp.where(token_segs[:, None] == seg_range[None, :], segment_step[None, :], 0), axis=1
    )
    step_range = jnp.arange(gain.shape[0], dtype=jnp.int32)
    step_hot = (seg_steps[:, None] == step_range[None, :]).astype(jnp.float32)
    row_gain = jnp.dot(step_hot, gain, precision=lax.Precision.HIGHEST)
    d_attn = (d_out.astype(jnp.float32) * row_gain).astype(jnp.bfloat16)
    head_q, head_k, head_v, head_d = (
        lax.all_to_all(queries, "head", split_axis=1, concat_axis=0, tiled=True),
        lax.all_to_all(keys, "head", split_axis=1, concat_axis=0, tiled=True),
        lax.all_to_all(values, "head", split_axis=1, concat_axis=0, tiled=True),
        lax.all_to_all(d_attn, "head", split_axis=1, concat_axis=0, tiled=True),
    )
    own_q = head_q.reshape(block_rows, local_heads, HD)
    own_d = head_d.reshape(block_rows, local_heads, HD)
    own_segs = segment_ids(
        my_slot * block_rows + jnp.arange(block_rows, dtype=jnp.int32), segment_lengths
    )
    group = math.gcd(seq_count, max(1, 512 // block_rows))
    step_rows = group * block_rows
    step_count = seq_count // group
    all_rows = jnp.arange(total_rows, dtype=jnp.int32)
    all_pos = slot_lookup(all_rows // block_rows, block_slot) * block_rows + all_rows % block_rows
    all_segs = segment_ids(all_pos, segment_lengths).reshape(step_count, step_rows)
    gathered_k, gathered_v = (
        lax.all_gather(head_k, "seq", axis=0, tiled=True),
        lax.all_gather(head_v, "seq", axis=0, tiled=True),
    )
    key_blocks = gathered_k.reshape(step_count, step_rows, local_heads, HD)
    value_blocks = gathered_v.reshape(step_count, step_rows, local_heads, HD)
    empty_rows = jnp.zeros((local_heads, block_rows), jnp.float32)
    start_stats = (empty_rows + NEGATIVE, empty_rows, empty_rows)

    def stats_step(carry, block):
        scores, d_probs, visible = pair_terms(
            own_q, own_d, block[0], block[1], own_segs, block[2], scaling
        )
        return (combine_stats(carry, partial_stats(scores, d_probs, visible)), 0)

    totals = lax.scan(stats_step, start_stats, (key_blocks, value_blocks, all_segs))[0]
    log_total = totals[0] + jnp.log(totals[1])
    delta = totals[2] / totals[1]

    def grad_step(carry, block):
        state = carry
        scores, d_probs, visible = pair_terms(
            own_q, own_d, block[0], block[1], own_segs, block[2], scaling
        )
        probs, shifted = grad_terms(scores, d_probs, visible, log_total, delta)
        state = state + scaling * jnp.einsum(
            "hqk,khd->qhd", shifted, block[0], preferred_element_type=jnp.float32
        )
        d_key = scaling * jnp.einsum(
            "hqk,qhd->khd", shifted, own_q, preferred_element_type=jnp.float32
        )
        d_value = jnp.einsum("hqk,qhd->khd", probs, own_d, preferred_element_type=jnp.float32)
        return (state, (d_key, d_value))

    start_query = jnp.zeros((block_rows, local_heads, HD), jnp.float32)
    d_query, key_terms = lax.scan(grad_step, start_query, (key_blocks, value_blocks, all_segs))
    d_key, d_value = (
        lax.psum_scatter(
            key_terms[0].reshape(total_rows, head_width), "seq", scatter_dimension=0, tiled=True
        ),
        lax.psum_scatter(
            key_terms[1].reshape(total_rows, head_width), "seq", scatter_dimension=0, tiled=True
        ),
    )
    d_query = d_query.reshape(block_rows, head_width)
    return (
        lax.all_to_all(
            d_query.astype(jnp.bfloat16), "head", split_axis=0, concat_axis=1, tiled=True
        ),
        lax.all_to_all(d_key.astype(jnp.bfloat16), "head", split_axis=0, concat_axis=1, tiled=True),
        lax.all_to_all(
            d_value.astype(jnp.bfloat16), "head", split_axis=0, concat_axis=1, tiled=True
        ),
    )


def solution(mesh):
    return jax.shard_map(
        shards,
        mesh=mesh,
        in_specs=(
            P(("seq", "head"), None),
            P(("seq", "head"), None),
            P(("seq", "head"), None),
            P(("seq", "head"), None),
            P(),
            P(),
            P(),
            P(),
        ),
        out_specs=(P(("seq", "head"), None), P(("seq", "head"), None), P(("seq", "head"), None)),
        check_vma=False,
    )
```

profile of v0, /device:TPU:8, one launch (start us, length us, event | category | flops | bytes accessed | tf_op | source)
XLA Modules:
  0.0 695.6 jit_solution(9260966016412313357)
XLA Ops:
  8.2 20.6 %all_to_all.124 = bf16[24,8,384]{2,0,1:T(8,128)(2,1)} all-to-all(bf16[24,8,384]{2,0,1:T(8,128)(2,1)S(1)} %bitcast.164), channel_id=1, replica_groups=mesh['seq'=32,'head'=8] {'head'}, dimensions={1} | all-to-all | bytes 294912 | tf_op jit(solution)/shard_map/all_to_all | solution.py:85
  29.8 13.7 %all_to_all.125 = bf16[24,8,384]{2,0,1:T(8,128)(2,1)} all-to-all(bf16[24,8,384]{2,0,1:T(8,128)(2,1)S(1)} %bitcast.165), channel_id=1, replica_groups=mesh['seq'=32,'head'=8] {'head'}, dimensions={1} | all-to-all | bytes 294912 | tf_op jit(solution)/shard_map/all_to_all | solution.py:84
  49.0 4.8 all-to-all-start.3
  56.4 7.4 %all-to-all-done.3 = bf16[24,8,384]{2,0,1:T(8,128)(2,1)S(1)} async-done(((bf16[24,8,384]{2,0,1:T(8,128)(2,1)}), bf16[24,8,384]{2,0,1:T(8,128)(2,1)S(1)}, u32[]{:S(2)}, u32[]{:S(2)}) %all-to-all-start.3) | async-done | bytes 147488 | tf_op jit(solution)/shard_map/all_to_all | solution.py:86
  63.8 5.1 all-to-all-start.1
  69.3 9.6 %all-to-all-done.1 = bf16[24,8,384]{2,0,1:T(8,128)(2,1)S(1)} async-done(((bf16[24,8,384]{2,0,1:T(8,128)(2,1)}), bf16[24,8,384]{2,0,1:T(8,128)(2,1)S(1)}, u32[]{:S(2)}, u32[]{:S(2)}) %all-to-all-start.1) | async-done | bytes 147488 | tf_op jit(solution)/shard_map/all_to_all | solution.py:83
  78.9 12.3 %all-gather.5.cloned.1.call-done = bf16[6144,384]{1,0:T(8,128)(2,1)} async-done(((bf16[192,384]{1,0:T(8,128)(2,1)}), bf16[6144,384]{1,0:T(8,128)(2,1)}) %all-gather.5.cloned.1.call-update) | async-done | bytes 4718608 | tf_op jit(solution)/shard_map/all_gather | solution.py:101
  91.2 13.0 %reshape.193 = bf16[16,384,3,128]{3,2,1,0:T(4,128)(2,1)} reshape(bf16[6144,384]{1,0:T(8,128)(2,1)} %all-gather.5.cloned.1.call-done) | data formatting | bytes 9437184 | tf_op jit(solution)/shard_map/reshape | solution.py:104
  104.2 6.3 copy.80
  110.5 46.4 %all-gather.3.cloned.1.call-done = bf16[6144,384]{1,0:T(8,128)(2,1)} async-done(((bf16[192,384]{1,0:T(8,128)(2,1)}), bf16[6144,384]{1,0:T(8,128)(2,1)}) %all-gather.3.cloned.1.call-update) | async-done | bytes 4718608 | tf_op jit(solution)/shard_map/all_gather | solution.py:100
  156.8 13.0 %reshape.192 = bf16[16,384,3,128]{3,2,1,0:T(4,128)(2,1)} reshape(bf16[6144,384]{1,0:T(8,128)(2,1)} %all-gather.3.cloned.1.call-done) | data formatting | bytes 9437184 | tf_op jit(solution)/shard_map/reshape | solution.py:103
  169.8 6.2 copy.82
  176.0 54.4 %while.30 = (s32[]{:T(128)}, f32[3,192]{1,0:T(4,128)S(1)}, f32[3,192]{1,0:T(4,128)S(1)}, f32[3,192]{1,0:T(4,128)S(1)}, s32[16,384]{1,0:T(8,128)S(1)}, /*index=5*...) while((s32[]{:T(128)}, f32[3,192]{1,0:T(4,128)S(1)}, ...), condition=%wide.region_11.12_spmd.clone, body=%wide.region_7.11_spmd.clone.sunk | while | flops 115538688 | bytes 3883156 | solution.py:114
  230.4 103.8 %while.31 = (s32[]{:T(128)}, f32[192,3,128]{2,0,1:T(8,128)S(1)}, f32[16,384,3,128]{3,1,2,0:T(8,128)}, f32[16,384,3,128]{3,1,2,0:T(8,128)}, bf16[16,384,3,128]{3,...) while((s32[]{:T(128)}, f32[192,3,128]{2,0,1:T(8,128)S(1)}, ...), condition=%wide.region_13.14_spmd.clone, body=%wide.region_12.13_spmd.clone.sunk | while | flops 285327360 | bytes 7382959 | solution.py:134
  334.3 12.9 %copy.103 = f32[16,384,3,128]{3,2,1,0:T(4,128)S(1)} copy(f32[16,384,3,128]{3,1,2,0:T(8,128)} %get-tuple-element.126) | data formatting | bytes 18874368
  347.2 4.8 copy.121
  352.3 12.9 %copy.102 = f32[16,384,3,128]{3,2,1,0:T(4,128)S(1)} copy(f32[16,384,3,128]{3,1,2,0:T(8,128)} %get-tuple-element.125) | data formatting | bytes 18874368
  365.2 4.8 copy.122
  371.0 8.5 %all-to-all-start.4 = ((bf16[8,24,384]{2,1,0:T(8,128)(2,1)}), bf16[8,24,384]{2,1,0:T(8,128)(2,1)S(1)}, u32[]{:S(2)}, u32[]{:S(2)}) async-start(bf16[8,24,384]{2,1,0:T(8,128)(2,1)} %convert_element_type.41), calls=%async_computation.4 | async-start | bytes 294912 | tf_op jit(solution)/shard_map/all_to_all | solution.py:145
  379.4 133.0 %reduce-scatter.9.cloned.1.call-done = f32[192,384]{1,0:T(8,128)} async-done(((f32[6144,384]{1,0:T(8,128)}), f32[192,384]{1,0:T(8,128)}) %reduce-scatter.9.cloned.1.call-update) | async-done | bytes 294928 | tf_op jit(solution)/shard_map/reduce_scatter | solution.py:139
  514.1 7.1 %all-to-all-start.6 = ((bf16[8,24,384]{2,1,0:T(8,128)(2,1)}), bf16[8,24,384]{2,1,0:T(8,128)(2,1)S(1)}, u32[]{:S(2)}, u32[]{:S(2)}) async-start(bf16[8,24,384]{2,1,0:T(8,128)(2,1)} %bitcast.11), calls=%async_computation.6 | async-start | bytes 294912 | tf_op jit(solution)/shard_map/all_to_all | solution.py:149
  521.2 150.4 %reduce-scatter.7.cloned.1.call-done = f32[192,384]{1,0:T(8,128)} async-done(((f32[6144,384]{1,0:T(8,128)}), f32[192,384]{1,0:T(8,128)}) %reduce-scatter.7.cloned.1.call-update) | async-done | bytes 294928 | tf_op jit(solution)/shard_map/reduce_scatter | solution.py:136
  673.2 6.2 all-to-all-start.5
  680.7 7.7 %all-to-all-done.5 = bf16[8,24,384]{2,1,0:T(8,128)(2,1)S(1)} async-done(((bf16[8,24,384]{2,1,0:T(8,128)(2,1)}), bf16[8,24,384]{2,1,0:T(8,128)(2,1)S(1)}, u32[]{:S(2)}, u32[]{:S(2)}) %all-to-all-start.5) | async-done | bytes 147488 | tf_op jit(solution)/shard_map/all_to_all | solution.py:148
  (290 shorter events, 173.4 us)
Async XLA Ops:
  7.2 40.0 %copy-start = (f32[16,3072]{1,0:T(8,128)S(1)}, f32[16,3072]{1,0:T(8,128)}, u32[]{:S(2)}) copy-start(f32[16,3072]{1,0:T(8,128)} %param.16) | copy-start | bytes 589828
  7.2 84.0 %all-gather.5.cloned.1.call-start = ((), (), s32[]{:S(2)}) async-start(), calls=%async_computation.10 | async-start | bytes 4866048 | tf_op jit(solution)/shard_map/all_gather | solution.py:101
  28.8 128.0 %all-gather.3.cloned.1.call-start = ((), (), s32[]{:S(2)}) async-start(), calls=%async_computation.9 | async-start | bytes 4866048 | tf_op jit(solution)/shard_map/all_gather | solution.py:100
  49.0 14.8 %all-to-all-start.3 = ((bf16[24,8,384]{2,0,1:T(8,128)(2,1)}), bf16[24,8,384]{2,0,1:T(8,128)(2,1)S(1)}, u32[]{:S(2)}, u32[]{:S(2)}) async-start(bf16[24,8,384]{2,0,1:T(8,128)(2,1)} %bitcast.112), calls=%async_computation.3 | async-start | bytes 294912 | tf_op jit(solution)/shard_map/all_to_all | solution.py:86
  63.8 15.0 %all-to-all-start.1 = ((bf16[24,8,384]{2,0,1:T(8,128)(2,1)}), bf16[24,8,384]{2,0,1:T(8,128)(2,1)S(1)}, u32[]{:S(2)}, u32[]{:S(2)}) async-start(bf16[24,8,384]{2,0,1:T(8,128)(2,1)} %bitcast.114), calls=%async_computation.1 | async-start | bytes 294912 | tf_op jit(solution)/shard_map/all_to_all | solution.py:83
  68.9 443.6 %reduce-scatter.9.cloned.1.call-start = ((), (), s32[]{:S(2)}) async-start(), calls=%async_computation.12 | async-start | bytes 9732096 | tf_op jit(solution)/shard_map/reduce_scatter | solution.py:139
  352.0 319.5 %reduce-scatter.7.cloned.1.call-start = ((), (), s32[]{:S(2)}) async-start(), calls=%async_computation.11 | async-start | bytes 9732096 | tf_op jit(solution)/shard_map/reduce_scatter | solution.py:136
  365.2 323.9 %copy-start.1 = (f32[16,3072]{1,0:T(8,128)S(1)}, f32[16,3072]{1,0:T(8,128)}, u32[]{:S(2)}) copy-start(f32[16,3072]{1,0:T(8,128)} %param.16) | copy-start | bytes 589828
  371.0 143.1 %all-to-all-start.4 = ((bf16[8,24,384]{2,1,0:T(8,128)(2,1)}), bf16[8,24,384]{2,1,0:T(8,128)(2,1)S(1)}, u32[]{:S(2)}, u32[]{:S(2)}) async-start(bf16[8,24,384]{2,1,0:T(8,128)(2,1)} %convert_element_type.41), calls=%async_computation.4 | async-start | bytes 294912 | tf_op jit(solution)/shard_map/all_to_all | solution.py:145
  514.1 159.1 %all-to-all-start.6 = ((bf16[8,24,384]{2,1,0:T(8,128)(2,1)}), bf16[8,24,384]{2,1,0:T(8,128)(2,1)S(1)}, u32[]{:S(2)}, u32[]{:S(2)}) async-start(bf16[8,24,384]{2,1,0:T(8,128)(2,1)} %bitcast.11), calls=%async_computation.6 | async-start | bytes 294912 | tf_op jit(solution)/shard_map/all_to_all | solution.py:149
  673.2 15.2 %all-to-all-start.5 = ((bf16[8,24,384]{2,1,0:T(8,128)(2,1)}), bf16[8,24,384]{2,1,0:T(8,128)(2,1)S(1)}, u32[]{:S(2)}, u32[]{:S(2)}) async-start(bf16[8,24,384]{2,1,0:T(8,128)(2,1)} %bitcast.9), calls=%async_computation.5 | async-start | bytes 294912 | tf_op jit(solution)/shard_map/all_to_all | solution.py:148
Sparse Core Ops, SparseCore 0:
  28.9 62.2 all-gather.4
  93.1 63.7 all-gather.2
  352.2 160.2 reduce-scatter.8
  514.8 156.6 reduce-scatter.6
where the time goes:
time: 700 us; the launch traced here: 696 us
  waiting for transfers between devices  367 us (52%)
  matrix products  147 us (21%)
  local copies, waits for them, and re-layouts  81.9 us (12%)
  blocking collectives  34.3 us (5%)
  starting transfers between devices  32 us (5%)
  other arithmetic  17.8 us (3%)
  between operations  14.6 us (2%)
    reduce_scatter x1, waiting for transfers between devices, shards(): lax.psum_scatter(key_terms[0].reshape(total_rows, head_width), 'seq', sca...  150 us
    reduce_scatter x1, waiting for transfers between devices, shards(): lax.psum_scatter(key_terms[1].reshape(total_rows, head_width), 'seq', sca...  133 us
    unnamed x12, local copies, waits for them, and re-layouts  48 us
    all_gather x1, waiting for transfers between devices, shards(): lax.all_gather(head_k, 'seq', axis=0, tiled=True)  46.4 us
    dot_general x32, matrix products, pair_terms(): jnp.einsum('qhd,khd->hqk', query_rows, key_rows, preferred_element_type=j...  43.8 us
    dot_general x32, matrix products, pair_terms(): jnp.einsum('qhd,khd->hqk', cotan_rows, value_rows, preferred_element_type...  42.9 us
    dot_general x16, matrix products, grad_step(): jnp.einsum('hqk,khd->qhd', shifted, block[0], preferred_element_type=jnp....  20.8 us
    all_to_all x1, blocking collectives, shards(): lax.all_to_all(values, 'head', split_axis=1, concat_axis=0, tiled=True)  20.6 us
  transfers between devices with their start and end apart: 9, of which 7 were waited for; matrix products, arithmetic and copies ran while one was open for 7% of the time, Pallas kernels for 0%

commit v1 on v0

v1 whole, which is shorter than its diff:
```python
import functools
import math

import jax
import jax.numpy as jnp
from jax import lax
from jax.experimental import pallas as pl
from jax.experimental.pallas import tpu as pltpu
from jax.sharding import Mesh
from jax.sharding import PartitionSpec as P

HD = 128
BLK = 192
TOKENS = 6144
SEGMENTS = 8
HEADS = 24
QROWS = 768
QG = 256
GROUPS = QROWS // QG
TK = 256
X = 4
ZLO = 4
CORES = 2
NEGATIVE = -1e30
SCALING = 1.0 / math.sqrt(HD)
EXP2_SCALE = SCALING * math.log2(math.e)
COLUMNS = ("zlo", "zhi", "y")
TOKEN_AXES = ("zlo", "x", "core", "zhi", "y")


def attend_kernel(
    place, slots, lengths, steps, q_hbm, d_hbm, gain_hbm, *refs
):
    chunks = refs[0:8]
    dq_hbm = refs[8]
    dkv_mine = refs[9:13]
    dkv_other = refs[13]
    (kv, kt, q_rows, d_rows, q_cols, d_cols, gain, q_ends, scores, d_probs, dkv, dkv_low, dq_cols, dq_rows, sems) = refs[14:]
    my_x, my_core, my_head = place[0], place[1], place[2]

    def slot_at(zlo, x, core):
        return slots[zlo * (X * CORES) + x * CORES + core]

    mine = [slot_at(b, my_x, my_core) for b in range(ZLO)]
    ranks = []
    for b in range(ZLO):
        rank = jnp.int32(0)
        for other in range(ZLO):
            if other != b:
                rank = rank + (mine[other] < mine[b]).astype(jnp.int32)
        ranks.append(rank)
    ordered = []
    for r in range(ZLO):
        value = jnp.int32(0)
        for b in range(ZLO):
            value = jnp.where(ranks[b] == r, mine[b], value)
        ordered.append(value)

    copies = []
    gain_copy = pltpu.make_async_copy(
        gain_hbm.at[:, pl.ds(pl.multiple_of(my_head * HD, HD), HD)], gain, sems.at[0]
    )
    gain_copy.start()
    for b in range(ZLO):
        row = pl.ds(pl.multiple_of(ranks[b] * BLK, BLK), BLK)
        copies.append(pltpu.make_async_copy(q_hbm.at[pl.ds(b * BLK, BLK)], q_rows.at[row], sems.at[1 + b]))
        copies.append(pltpu.make_async_copy(d_hbm.at[pl.ds(b * BLK, BLK)], d_rows.at[row], sems.at[5 + b]))
    kv_copies = []
    for c in range(CORES):
        for s in range(X):
            for b in range(ZLO):
                slot = slot_at(b, (my_x + X - s) % X, (my_core + c) % CORES)
                kv_copies.append(
                    pltpu.make_async_copy(
                        chunks[c * X + s].at[pl.ds(b * BLK, BLK)],
                        kv.at[pl.ds(pl.multiple_of(slot * BLK, BLK), BLK)],
                        sems.at[9 + (c * X + s) * ZLO + b],
                    )
                )
    for copy in copies + kv_copies:
        copy.start()

    starts, ends = [], []
    total = jnp.int32(0)
    for s in range(SEGMENTS):
        starts.append(total)
        total = total + lengths[s]
        ends.append(total)

    def end_of(position):
        return sum(jnp.where(starts[s] <= position, lengths[s], 0) for s in range(SEGMENTS))

    def positions(shape, dimension):
        index = lax.broadcasted_iota(jnp.int32, shape, dimension)
        base = jnp.where(index < BLK, ordered[0] * BLK, ordered[1] * BLK - BLK)
        base = jnp.where(index < 2 * BLK, base, ordered[2] * BLK - 2 * BLK)
        base = jnp.where(index < 3 * BLK, base, ordered[3] * BLK - 3 * BLK)
        return base + index

    q_ends[...] = end_of(positions((1, QROWS), 1))
    dkv[...] = jnp.zeros_like(dkv)

    gain_copy.wait()
    for copy in copies:
        copy.wait()
    q_cols[...] = q_rows[...].T
    row_positions = positions((QROWS, HD), 0)
    row_gain = jnp.zeros((QROWS, HD), jnp.float32)
    for s in range(SEGMENTS):
        inside = (starts[s] <= row_positions) & (row_positions < ends[s])
        row_gain = jnp.where(inside, gain[pl.ds(steps[s], 1), :], row_gain)
    d_rows[...] = (d_rows[...].astype(jnp.float32) * row_gain).astype(jnp.bfloat16)
    d_cols[...] = d_rows[...].T
    for copy in kv_copies:
        copy.wait()
    for t in range(TOKENS // TK):
        kt[:, pl.ds(t * TK, TK)] = kv[pl.ds(t * TK, TK), 0:HD].T

    for g in range(GROUPS):
        lanes = slice(g * QG, (g + 1) * QG)
        first = ordered[g * QG // BLK] * BLK + g * QG % BLK
        last = ordered[((g + 1) * QG - 1) // BLK] * BLK + ((g + 1) * QG - 1) % BLK
        whole_tiles = end_of(first) // TK
        tiles = (end_of(last) + TK - 1) // TK
        qt = q_cols[:, lanes]
        dt = d_cols[:, lanes]
        limit = q_ends[:, lanes]

        def score_tile(t, top, masked):
            at = pl.ds(pl.multiple_of(t * TK, TK), TK)
            s = jnp.dot(kv[at, 0:HD], qt, preferred_element_type=jnp.float32)
            if masked:
                key_position = t * TK + lax.broadcasted_iota(jnp.int32, (TK, QG), 0)
                s = jnp.where(key_position < limit, s, NEGATIVE)
            scores[at, :] = s
            return jnp.maximum(top, jnp.max(s.reshape(TK // 8, 8, QG), axis=0))

        top = jnp.full((8, QG), NEGATIVE, jnp.float32)
        top = lax.fori_loop(0, whole_tiles, functools.partial(score_tile, masked=False), top)
        top = lax.fori_loop(whole_tiles, tiles, functools.partial(score_tile, masked=True), top)
        top = jnp.max(top, axis=0, keepdims=True)

        def weight_tile(t, carry):
            weight_sum, product_sum = carry
            at = pl.ds(pl.multiple_of(t * TK, TK), TK)
            w = jnp.exp2((scores[at, :] - top) * EXP2_SCALE)
            dp = jnp.dot(kv[at, HD:], dt, preferred_element_type=jnp.float32)
            scores[at, :] = w
            d_probs[at, :] = dp
            weight_sum = weight_sum + jnp.sum(w.reshape(TK // 8, 8, QG), axis=0)
            product_sum = product_sum + jnp.sum((w * dp).reshape(TK // 8, 8, QG), axis=0)
            return weight_sum, product_sum

        empty = jnp.zeros((8, QG), jnp.float32)
        weight_sum, product_sum = lax.fori_loop(0, tiles, weight_tile, (empty, empty))
        inverse = 1.0 / jnp.sum(weight_sum, axis=0, keepdims=True)
        delta = jnp.sum(product_sum, axis=0, keepdims=True) * inverse
        dq_cols[...] = jnp.zeros_like(dq_cols)
        q_part = q_rows[lanes, :]
        d_part = d_rows[lanes, :]

        def grad_tile(t, carry):
            at = pl.ds(pl.multiple_of(t * TK, TK), TK)
            p = scores[at, :] * inverse
            shifted = (p * (d_probs[at, :] - delta)).astype(jnp.bfloat16)
            dkv[at, HD:] += jnp.dot(p.astype(jnp.bfloat16), d_part, preferred_element_type=jnp.float32)
            dkv[at, 0:HD] += jnp.dot(shifted, q_part, preferred_element_type=jnp.float32)
            dq_cols[...] += jnp.dot(kt[:, at], shifted, preferred_element_type=jnp.float32)
            return carry

        lax.fori_loop(0, tiles, grad_tile, 0)
        dq_rows[lanes, :] = (dq_cols[...].T * SCALING).astype(jnp.bfloat16)

    dkv_low[:, 0:HD] = (dkv[:, 0:HD] * SCALING).astype(jnp.bfloat16)
    dkv_low[:, HD:] = dkv[:, HD:].astype(jnp.bfloat16)
    out_copies = []
    for b in range(ZLO):
        row = pl.ds(pl.multiple_of(ranks[b] * BLK, BLK), BLK)
        out_copies.append(pltpu.make_async_copy(dq_rows.at[row], dq_hbm.at[pl.ds(b * BLK, BLK)], sems.at[1 + b]))
    for c in range(CORES):
        for s in range(X):
            for b in range(ZLO):
                slot = slot_at(b, (my_x + s) % X, (my_core + c) % CORES)
                target = dkv_mine[s] if c == 0 else dkv_other.at[s]
                out_copies.append(
                    pltpu.make_async_copy(
                        dkv_low.at[pl.ds(pl.multiple_of(slot * BLK, BLK), BLK)],
                        target.at[pl.ds(b * BLK, BLK)],
                        sems.at[9 + (c * X + s) * ZLO + b],
                    )
                )
    for copy in out_copies:
        copy.start()
    for copy in out_copies:
        copy.wait()


def attend(place, slots, lengths, steps, q, d, gain, chunks):
    smem = pl.BlockSpec(memory_space=pltpu.SMEM)
    hbm = pl.BlockSpec(memory_space=pl.ANY)
    low = jnp.bfloat16
    outs = (
        [jax.ShapeDtypeStruct((QROWS, HD), low)]
        + [jax.ShapeDtypeStruct((QROWS, 2 * HD), low)] * X
        + [jax.ShapeDtypeStruct((X, QROWS, 2 * HD), low)]
    )
    return pl.pallas_call(
        attend_kernel,
        out_shape=outs,
        in_specs=[smem] * 4 + [hbm] * (3 + len(chunks)),
        out_specs=[hbm] * len(outs),
        scratch_shapes=[
            pltpu.VMEM((TOKENS, 2 * HD), low),
            pltpu.VMEM((HD, TOKENS), low),
            pltpu.VMEM((QROWS, HD), low),
            pltpu.VMEM((QROWS, HD), low),
            pltpu.VMEM((HD, QROWS), low),
            pltpu.VMEM((HD, QROWS), low),
            pltpu.VMEM((16, HD), jnp.float32),
            pltpu.VMEM((1, QROWS), jnp.int32),
            pltpu.VMEM((TOKENS, QG), jnp.float32),
            pltpu.VMEM((TOKENS, QG), jnp.float32),
            pltpu.VMEM((TOKENS, 2 * HD), jnp.float32),
            pltpu.VMEM((TOKENS, 2 * HD), low),
            pltpu.VMEM((HD, QG), jnp.float32),
            pltpu.VMEM((QROWS, HD), low),
            pltpu.SemaphoreType.DMA((9 + TOKENS // BLK,)),
        ],
        compiler_params=pltpu.CompilerParams(vmem_limit_bytes=48 * 1024 * 1024),
    )(place, slots, lengths, steps, q, d, gain, *chunks)


def x_shift(array, shift):
    return lax.ppermute(array, "x", [(i, (i + shift) % X) for i in range(X)])


def other_core(array):
    return lax.ppermute(array, "core", [(0, 1), (1, 0)])


def by_head(*arrays):
    rows = arrays[0].shape[0]
    parts = [a.reshape(rows, HEADS, HD).transpose(1, 0, 2) for a in arrays]
    joined = jnp.concatenate(parts, axis=2)
    return jnp.pad(joined, ((0, 32 - HEADS), (0, 0), (0, 0)))


def exchange(array):
    return lax.all_to_all(array, COLUMNS, split_axis=0, concat_axis=0, tiled=True)


def by_token(array, rows):
    return array[:HEADS].transpose(1, 0, 2).reshape(rows, HEADS * HD)


def shards(queries, keys, values, d_out, gain, lengths, steps, slots):
    rows = queries.shape[0]
    column = lax.axis_index("zlo") * 8 + lax.axis_index("zhi") * 4 + lax.axis_index("y")
    head = jnp.minimum(column, HEADS - 1)
    place = jnp.stack([lax.axis_index("x"), lax.axis_index("core"), head]).astype(jnp.int32)
    kv = exchange(by_head(keys, values)).reshape(QROWS, 2 * HD)
    q = exchange(by_head(queries)).reshape(QROWS, HD)
    d = exchange(by_head(d_out)).reshape(QROWS, HD)
    own = [kv] + [x_shift(kv, s) for s in range(1, X)]
    chunks = own + [other_core(c) for c in own]
    outs = attend(place, slots, lengths, steps, q, d, gain, chunks)
    dq, mine, other = outs[0], outs[1:5], outs[5]
    received = other_core(other)
    pair = [
        (mine[s].astype(jnp.float32) + received[s].astype(jnp.float32)).astype(jnp.bfloat16)
        for s in range(X)
    ]
    total = pair[0].astype(jnp.float32)
    for s in range(1, X):
        total = total + x_shift(pair[s], s).astype(jnp.float32)
    dq = exchange(dq.reshape(32, rows, HD))
    dkv = exchange(total.astype(jnp.bfloat16).reshape(32, rows, 2 * HD))
    return by_token(dq, rows), by_token(dkv[..., :HD], rows), by_token(dkv[..., HD:], rows)


def solution(mesh):
    split = Mesh(mesh.devices.reshape(ZLO, X, CORES, 2, 4), TOKEN_AXES)
    tokens = P(TOKEN_AXES, None)
    return jax.shard_map(
        shards,
        mesh=split,
        in_specs=(tokens,) * 4 + (P(),) * 4,
        out_specs=(tokens,) * 3,
        check_vma=False,
    )
```

time: 700 us -> 166 us (0.24)
  the two profiles are of different devices: /device:TPU:8 before, /device:TPU:32 now
where the time goes in v1:
time: 166 us; the launch traced here: 164 us
  waiting for transfers between devices  51.9 us (31%)
  Pallas kernels  44.9 us (27%)
  starting transfers between devices  30.5 us (18%)
  blocking collectives  26.7 us (16%)
  local copies, waits for them, and re-layouts  5.43 us (3%)
  other arithmetic  3.31 us (2%)
    pallas_call x1, Pallas kernels, attend(): pl.pallas_call(attend_kernel, out_shape=outs, in_specs=[smem] * 4 + [hbm]...  44.9 us
    all_to_all x1, blocking collectives, exchange(): lax.all_to_all(array, COLUMNS, split_axis=0, concat_axis=0, tiled=True)  26.7 us
    all_to_all x4, waiting for transfers between devices, exchange(): lax.all_to_all(array, COLUMNS, split_axis=0, concat_axis=0, tiled=True)  26.2 us
    ppermute x6, waiting for transfers between devices, x_shift(): return lax.ppermute(array, 'x', [(i, (i + shift) % X) for i in range(X)])  22.1 us
    all_to_all x4, starting transfers between devices, exchange(): lax.all_to_all(array, COLUMNS, split_axis=0, concat_axis=0, tiled=True)  18.8 us
    ppermute x6, starting transfers between devices, x_shift(): return lax.ppermute(array, 'x', [(i, (i + shift) % X) for i in range(X)])  10.9 us
    ppermute x5, waiting for transfers between devices, other_core(): return lax.ppermute(array, 'core', [(0, 1), (1, 0)])  3.62 us
  transfers between devices with their start and end apart: 15, of which 7 were waited for; matrix products, arithmetic and copies ran while one was open for 3% of the time, Pallas kernels for 0%

profile of v1, /device:TPU:32, one launch (start us, length us, event | category | flops | bytes accessed | tf_op | source)
XLA Modules:
  0.0 163.6 jit_solution(8060075017843449594)
XLA Ops:
  0.7 0.9 copy-done
  1.5 1.0 bitcast_bitcast_fusion
  2.6 26.7 %all_to_all.25 = bf16[32,24,256]{2,1,0:T(8,128)(2,1)S(1)} all-to-all(bf16[32,24,256]{2,1,0:T(8,128)(2,1)S(1)} %fusion.6), channel_id=1, replica_groups=mesh['zlo'=4,'x'=4,'core'=2,'zhi'=2,'y'=4] {'zlo','zhi','y'}, dimensions={0} | all-to-all | bytes 786432 | tf_op jit(solution)/shard_map/all_to_all | solution.py:249
  29.3 2.8 %collective-permute-start.2 = (bf16[768,256]{1,0:T(8,128)(2,1)S(1)}, bf16[768,256]{1,0:T(8,128)(2,1)S(1)}, u32[]{:S(2)}, u32[]{:S(2)}) collective-permute-start(bf16[768,256]{1,0:T(8,128)(2,1)S(1)} %bitcast.74), channel_id=1, source_target_pairs={{0,48},{16,0},{32,16},{48,32},{1,49},{17,1},{33,17},{49,33},{2,50}... | collective-permute-start | bytes 1179656 | tf_op jit(solution)/shard_map/ppermute | solution.py:234
  32.0 0.8 collective-permute-start.1
  32.8 0.9 collective-permute-start
  33.8 0.7 pad.11
  34.5 4.3 %all-to-all-start = ((bf16[32,24,128]{2,1,0:T(8,128)(2,1)}), bf16[32,24,128]{2,1,0:T(8,128)(2,1)S(1)}, u32[]{:S(2)}, u32[]{:S(2)}) async-start(bf16[32,24,128]{2,1,0:T(8,128)(2,1)} %pad.11), calls=%async_computation | async-start | bytes 393216 | tf_op jit(solution)/shard_map/all_to_all | solution.py:249
  38.9 8.4 %collective-permute-done.2.refs_3_ = bf16[768,256]{1,0:T(8,128)(2,1)S(1)} collective-permute-done((bf16[768,256]{1,0:T(8,128)(2,1)S(1)}, bf16[768,256]{1,0:T(8,128)(2,1)S(1)}, u32[]{:S(2)}, u32[]{:S(2)}) %collective-permute-start.2) | collective-permute-done | bytes 393248 | tf_op jit(solution)/shard_map/ppermute | solution.py:234
  47.8 3.2 %collective-permute-done.refs_1_ = bf16[768,256]{1,0:T(8,128)(2,1)S(1)} collective-permute-done((bf16[768,256]{1,0:T(8,128)(2,1)S(1)}, bf16[768,256]{1,0:T(8,128)(2,1)S(1)}, u32[]{:S(2)}, u32[]{:S(2)}) %collective-permute-start) | collective-permute-done | bytes 393248 | tf_op jit(solution)/shard_map/ppermute | solution.py:234
  51.0 0.7 pad.12
  51.7 5.4 %all-to-all-start.1 = ((bf16[32,24,128]{2,1,0:T(8,128)(2,1)}), bf16[32,24,128]{2,1,0:T(8,128)(2,1)S(1)}, u32[]{:S(2)}, u32[]{:S(2)}) async-start(bf16[32,24,128]{2,1,0:T(8,128)(2,1)} %pad.12), calls=%async_computation.1 | async-start | bytes 393216 | tf_op jit(solution)/shard_map/all_to_all | solution.py:249
  57.1 11.8 %all-to-all-done.1 = bf16[32,24,128]{2,1,0:T(8,128)(2,1)S(1)} async-done(((bf16[32,24,128]{2,1,0:T(8,128)(2,1)}), bf16[32,24,128]{2,1,0:T(8,128)(2,1)S(1)}, u32[]{:S(2)}, u32[]{:S(2)}) %all-to-all-start.1) | async-done | bytes 196640 | tf_op jit(solution)/shard_map/all_to_all | solution.py:249
  69.0 44.9 %shard_map.103 = (bf16[768,128]{1,0:T(8,128)(2,1)S(1)}, bf16[768,256]{1,0:T(8,128)(2,1)S(1)}, bf16[768,256]{1,0:T(8,128)(2,1)S(1)}, bf16[768,256]{1,0:T(8,128)(2...) custom-call(s32[3]{0:T(128)S(1)} %pad_add_fusion.place, s32[32]{0:T(128)S(1)} %copy-done.4, ...), custom_call_target="tpu_custom_call" | custom-call | tf_op jit(solution)/shard_map/pallas_call | solution.py:207
  114.0 3.6 %collective-permute-done.7 = bf16[4,768,256]{2,1,0:T(8,128)(2,1)S(1)} collective-permute-done((bf16[4,768,256]{2,1,0:T(8,128)(2,1)}, bf16[4,768,256]{2,1,0:T(8,128)(2,1)S(1)}, u32[]{:S(2)}, u32[]{:S(2)}) %collective-permute-start.7) | collective-permute-done | bytes 1572896 | tf_op jit(solution)/shard_map/ppermute | solution.py:238
  117.6 1.1 fusion.4
  118.7 4.3 %collective-permute-start.8 = (bf16[768,256]{1,0:T(8,128)(2,1)}, bf16[768,256]{1,0:T(8,128)(2,1)S(1)}, u32[]{:S(2)}, u32[]{:S(2)}) collective-permute-start(bf16[768,256]{1,0:T(8,128)(2,1)} %get-tuple-element.15), channel_id=1, source_target_pairs={{0,16},{16,32},{32,48},{48,0},{1,17},{17,33},{33,49},{49,1},{2,18}... | collective-permute-start | bytes 1179656 | tf_op jit(solution)/shard_map/ppermute | solution.py:234
  123.0 2.1 %collective-permute-start.9 = (bf16[768,256]{1,0:T(8,128)(2,1)S(1)}, bf16[768,256]{1,0:T(8,128)(2,1)}, u32[]{:S(2)}, u32[]{:S(2)}) collective-permute-start(bf16[768,256]{1,0:T(8,128)(2,1)S(1)} %get-tuple-element.17), channel_id=1, source_target_pairs={{0,32},{16,48},{32,0},{48,16},{1,33},{17,49},{33,1},{49,17},{2,34}... | collective-permute-start | bytes 1179656 | tf_op jit(solution)/shard_map/ppermute | solution.py:234
  125.2 4.6 %all-to-all-start.3 = ((bf16[32,24,128]{2,1,0:T(8,128)(2,1)}), bf16[32,24,128]{2,1,0:T(8,128)(2,1)S(1)}, u32[]{:S(2)}, u32[]{:S(2)}) async-start(bf16[32,24,128]{2,1,0:T(8,128)(2,1)} %bitcast.81), calls=%async_computation.3 | async-start | bytes 393216 | tf_op jit(solution)/shard_map/all_to_all | solution.py:249
  129.8 9.9 %collective-permute-done.8 = bf16[768,256]{1,0:T(8,128)(2,1)S(1)} collective-permute-done((bf16[768,256]{1,0:T(8,128)(2,1)}, bf16[768,256]{1,0:T(8,128)(2,1)S(1)}, u32[]{:S(2)}, u32[]{:S(2)}) %collective-permute-start.8) | collective-permute-done | bytes 393248 | tf_op jit(solution)/shard_map/ppermute | solution.py:234
  140.3 2.1 %add_convert_fusion = bf16[768,256]{1,0:T(8,128)(2,1)} fusion(bf16[768,256]{1,0:T(8,128)(2,1)S(1)} %collective-permute-done.10, bf16[768,256]{1,0:T(8,128)(2,1)} %collective-permute-done.9, bf16[768,256]{1,0:T(8,128)(2,1)S(1)} %collective-permute-done.8, bf16[768,256]{1,0:T(8,128)(2,1)} %copy-done.1, bf16[4,768,256]{2,1,0:T(8,128)(2,1)S(1)} %collective-permute-done.7), kind=kLoop, calls=%fused_computation.11 | loop fusion | flops 2359296 | bytes 2359296 | tf_op jit(solution)/shard_map/convert_element_type | solution.py:277
  142.5 4.6 %all-to-all-start.4 = ((bf16[32,24,256]{2,1,0:T(8,128)(2,1)}), bf16[32,24,256]{2,1,0:T(8,128)(2,1)S(1)}, u32[]{:S(2)}, u32[]{:S(2)}) async-start(bf16[32,24,256]{2,1,0:T(8,128)(2,1)} %bitcast.16), calls=%async_computation.4 | async-start | bytes 786432 | tf_op jit(solution)/shard_map/all_to_all | solution.py:249
  147.8 14.4 %all-to-all-done.4 = bf16[32,24,256]{2,1,0:T(8,128)(2,1)S(1)} async-done(((bf16[32,24,256]{2,1,0:T(8,128)(2,1)}), bf16[32,24,256]{2,1,0:T(8,128)(2,1)S(1)}, u32[]{:S(2)}, u32[]{:S(2)}) %all-to-all-start.4) | async-done | bytes 393248 | tf_op jit(solution)/shard_map/all_to_all | solution.py:249
  162.2 0.7 copy.32
  (39 shorter events, 3.0 us)
Async XLA Ops:
  0.6 0.9 copy-start
  0.6 33.1 %copy-start.7 = (bf16[24,3072]{1,0:T(8,128)(2,1)S(1)}, bf16[24,3072]{1,0:T(8,128)(2,1)}, u32[]{:S(2)}) copy-start(bf16[24,3072]{1,0:T(8,128)(2,1)} %param.8) | copy-start | bytes 442372
  0.7 50.3 %copy-start.8 = (bf16[24,3072]{1,0:T(8,128)(2,1)S(1)}, bf16[24,3072]{1,0:T(8,128)(2,1)}, u32[]{:S(2)}) copy-start(bf16[24,3072]{1,0:T(8,128)(2,1)} %param.11) | copy-start | bytes 442372
  2.6 66.4 %copy-start.2 = (f32[16,3072]{1,0:T(8,128)S(1)}, f32[16,3072]{1,0:T(8,128)}, u32[]{:S(2)}) copy-start(f32[16,3072]{1,0:T(8,128)} %gain_hbm.1) | copy-start | bytes 589828
  2.6 66.4 %copy-start.4 = (s32[32]{0:T(128)S(1)}, s32[32]{0:T(128)}, u32[]{:S(2)}) copy-start(s32[32]{0:T(128)} %slots.1) | copy-start | bytes 388
  2.6 66.4 %copy-start.5 = (s32[8]{0:T(128)S(1)}, s32[8]{0:T(128)}, u32[]{:S(2)}) copy-start(s32[8]{0:T(128)} %lengths.1) | copy-start | bytes 100
  2.6 66.4 %copy-start.6 = (s32[8]{0:T(128)S(1)}, s32[8]{0:T(128)}, u32[]{:S(2)}) copy-start(s32[8]{0:T(128)} %steps.1) | copy-start | bytes 100
  29.3 18.0 %collective-permute-start.2 = (bf16[768,256]{1,0:T(8,128)(2,1)S(1)}, bf16[768,256]{1,0:T(8,128)(2,1)S(1)}, u32[]{:S(2)}, u32[]{:S(2)}) collective-permute-start(bf16[768,256]{1,0:T(8,128)(2,1)S(1)} %bitcast.74), channel_id=1, source_target_pairs={{0,48},{16,0},{32,16},{48,32},{1,49},{17,1},{33,17},{49,33},{2,50}... | collective-permute-start | bytes 1179656 | tf_op jit(solution)/shard_map/ppermute | solution.py:234
  32.0 15.2 %collective-permute-start.1 = (bf16[768,256]{1,0:T(8,128)(2,1)S(1)}, bf16[768,256]{1,0:T(8,128)(2,1)S(1)}, u32[]{:S(2)}, u32[]{:S(2)}) collective-permute-start(bf16[768,256]{1,0:T(8,128)(2,1)S(1)} %bitcast.75), channel_id=1, source_target_pairs={{0,32},{16,48},{32,0},{48,16},{1,33},{17,49},{33,1},{49,17},{2,34}... | collective-permute-start | bytes 1179656 | tf_op jit(solution)/shard_map/ppermute | solution.py:234
  32.8 18.1 %collective-permute-start = (bf16[768,256]{1,0:T(8,128)(2,1)S(1)}, bf16[768,256]{1,0:T(8,128)(2,1)S(1)}, u32[]{:S(2)}, u32[]{:S(2)}) collective-permute-start(bf16[768,256]{1,0:T(8,128)(2,1)S(1)} %bitcast.76), channel_id=1, source_target_pairs={{0,16},{16,32},{32,48},{48,0},{1,17},{17,33},{33,49},{49,1},{2,18}... | collective-permute-start | bytes 1179656 | tf_op jit(solution)/shard_map/ppermute | solution.py:234
  34.5 17.2 %all-to-all-start = ((bf16[32,24,128]{2,1,0:T(8,128)(2,1)}), bf16[32,24,128]{2,1,0:T(8,128)(2,1)S(1)}, u32[]{:S(2)}, u32[]{:S(2)}) async-start(bf16[32,24,128]{2,1,0:T(8,128)(2,1)} %pad.11), calls=%async_computation | async-start | bytes 393216 | tf_op jit(solution)/shard_map/all_to_all | solution.py:249
  38.8 30.2 %collective-permute-start.3 = (bf16[768,256]{1,0:T(8,128)(2,1)S(1)}, bf16[768,256]{1,0:T(8,128)(2,1)S(1)}, u32[]{:S(2)}, u32[]{:S(2)}) collective-permute-start(bf16[768,256]{1,0:T(8,128)(2,1)S(1)} %bitcast.77), channel_id=1, source_target_pairs={{0,8},{8,0},{1,9},{9,1},{2,10},{10,2},{3,11},{11,3},{4,12},{12,4},... | collective-permute-start | bytes 1179656 | tf_op jit(solution)/shard_map/ppermute | solution.py:238
  47.2 21.7 %collective-permute-start.6 = (bf16[768,256]{1,0:T(8,128)(2,1)S(1)}, bf16[768,256]{1,0:T(8,128)(2,1)S(1)}, u32[]{:S(2)}, u32[]{:S(2)}) collective-permute-start(bf16[768,256]{1,0:T(8,128)(2,1)S(1)} %collective-permute-done.2.refs_3_), channel_id=1, source_target_pairs={{0,8},{8,0},{1,9},{9,1},{2,10},{10,2},{3,11},{11,3},{4,12},{12,4},... | collective-permute-start | bytes 1179656 | tf_op jit(solution)/shard_map/ppermute | solution.py:238
  47.2 21.7 %collective-permute-start.5 = (bf16[768,256]{1,0:T(8,128)(2,1)S(1)}, bf16[768,256]{1,0:T(8,128)(2,1)S(1)}, u32[]{:S(2)}, u32[]{:S(2)}) collective-permute-start(bf16[768,256]{1,0:T(8,128)(2,1)S(1)} %collective-permute-done.1.refs_2_), channel_id=1, source_target_pairs={{0,8},{8,0},{1,9},{9,1},{2,10},{10,2},{3,11},{11,3},{4,12},{12,4},... | collective-permute-start | bytes 1179656 | tf_op jit(solution)/shard_map/ppermute | solution.py:238
  50.9 18.0 %collective-permute-start.4 = (bf16[768,256]{1,0:T(8,128)(2,1)S(1)}, bf16[768,256]{1,0:T(8,128)(2,1)}, u32[]{:S(2)}, u32[]{:S(2)}) collective-permute-start(bf16[768,256]{1,0:T(8,128)(2,1)S(1)} %collective-permute-done.refs_1_), channel_id=1, source_target_pairs={{0,8},{8,0},{1,9},{9,1},{2,10},{10,2},{3,11},{11,3},{4,12},{12,4},... | collective-permute-start | bytes 1179656 | tf_op jit(solution)/shard_map/ppermute | solution.py:238
  51.7 17.3 %all-to-all-start.1 = ((bf16[32,24,128]{2,1,0:T(8,128)(2,1)}), bf16[32,24,128]{2,1,0:T(8,128)(2,1)S(1)}, u32[]{:S(2)}, u32[]{:S(2)}) async-start(bf16[32,24,128]{2,1,0:T(8,128)(2,1)} %pad.12), calls=%async_computation.1 | async-start | bytes 393216 | tf_op jit(solution)/shard_map/all_to_all | solution.py:249
  113.9 4.8 %copy-start.1 = (bf16[768,256]{1,0:T(8,128)(2,1)}, bf16[768,256]{1,0:T(8,128)(2,1)S(1)}, u32[]{:S(2)}) copy-start(bf16[768,256]{1,0:T(8,128)(2,1)S(1)} %get-tuple-element.10) | copy-start | bytes 1179652
  113.9 4.8 %copy-start.3 = (bf16[768,128]{1,0:T(8,128)(2,1)}, bf16[768,128]{1,0:T(8,128)(2,1)S(1)}, u32[]{:S(2)}) copy-start(bf16[768,128]{1,0:T(8,128)(2,1)S(1)} %get-tuple-element.9) | copy-start | bytes 589828
  113.9 3.7 %collective-permute-start.7 = (bf16[4,768,256]{2,1,0:T(8,128)(2,1)}, bf16[4,768,256]{2,1,0:T(8,128)(2,1)S(1)}, u32[]{:S(2)}, u32[]{:S(2)}) collective-permute-start(bf16[4,768,256]{2,1,0:T(8,128)(2,1)} %get-tuple-element.11), channel_id=1, source_target_pairs={{0,8},{8,0},{1,9},{9,1},{2,10},{10,2},{3,11},{11,3},{4,12},{12,4},... | collective-permute-start | bytes 4718600 | tf_op jit(solution)/shard_map/ppermute | solution.py:238
  118.7 21.0 %collective-permute-start.8 = (bf16[768,256]{1,0:T(8,128)(2,1)}, bf16[768,256]{1,0:T(8,128)(2,1)S(1)}, u32[]{:S(2)}, u32[]{:S(2)}) collective-permute-start(bf16[768,256]{1,0:T(8,128)(2,1)} %get-tuple-element.15), channel_id=1, source_target_pairs={{0,16},{16,32},{32,48},{48,0},{1,17},{17,33},{33,49},{49,1},{2,18}... | collective-permute-start | bytes 1179656 | tf_op jit(solution)/shard_map/ppermute | solution.py:234
  123.0 16.7 %collective-permute-start.10 = (bf16[768,256]{1,0:T(8,128)(2,1)S(1)}, bf16[768,256]{1,0:T(8,128)(2,1)S(1)}, u32[]{:S(2)}, u32[]{:S(2)}) collective-permute-start(bf16[768,256]{1,0:T(8,128)(2,1)S(1)} %get-tuple-element.16), channel_id=1, source_target_pairs={{0,48},{16,0},{32,16},{48,32},{1,49},{17,1},{33,17},{49,33},{2,50}... | collective-permute-start | bytes 1179656 | tf_op jit(solution)/shard_map/ppermute | solution.py:234
  123.0 17.3 %collective-permute-start.9 = (bf16[768,256]{1,0:T(8,128)(2,1)S(1)}, bf16[768,256]{1,0:T(8,128)(2,1)}, u32[]{:S(2)}, u32[]{:S(2)}) collective-permute-start(bf16[768,256]{1,0:T(8,128)(2,1)S(1)} %get-tuple-element.17), channel_id=1, source_target_pairs={{0,32},{16,48},{32,0},{48,16},{1,33},{17,49},{33,1},{49,17},{2,34}... | collective-permute-start | bytes 1179656 | tf_op jit(solution)/shard_map/ppermute | solution.py:234
  125.2 17.3 %all-to-all-start.3 = ((bf16[32,24,128]{2,1,0:T(8,128)(2,1)}), bf16[32,24,128]{2,1,0:T(8,128)(2,1)S(1)}, u32[]{:S(2)}, u32[]{:S(2)}) async-start(bf16[32,24,128]{2,1,0:T(8,128)(2,1)} %bitcast.81), calls=%async_computation.3 | async-start | bytes 393216 | tf_op jit(solution)/shard_map/all_to_all | solution.py:249
  142.5 19.7 %all-to-all-start.4 = ((bf16[32,24,256]{2,1,0:T(8,128)(2,1)}), bf16[32,24,256]{2,1,0:T(8,128)(2,1)S(1)}, u32[]{:S(2)}, u32[]{:S(2)}) async-start(bf16[32,24,256]{2,1,0:T(8,128)(2,1)} %bitcast.16), calls=%async_computation.4 | async-start | bytes 786432 | tf_op jit(solution)/shard_map/all_to_all | solution.py:249

commit v2 on v1

v2 whole, which is shorter than its diff:
```python
import functools
import math

import jax
import jax.numpy as jnp
from jax import lax
from jax.experimental import pallas as pl
from jax.experimental.pallas import tpu as pltpu
from jax.sharding import Mesh
from jax.sharding import PartitionSpec as P

HD = 128
BLK = 192
TOKENS = 6144
SEGMENTS = 8
HEADS = 24
QROWS = 768
QG = 384
GROUPS = QROWS // QG
TK = 768
PARTS = 2
TP = TK // PARTS
X = 4
ZLO = 4
CORES = 2
NEGATIVE = -1e30
SCALING = 1.0 / math.sqrt(HD)
EXP2_SCALE = SCALING * math.log2(math.e)
COLUMNS = ("zlo", "zhi", "y")
TOKEN_AXES = ("zlo", "x", "core", "zhi", "y")


def place():
    column = lax.axis_index("zlo") * 8 + lax.axis_index("zhi") * 4 + lax.axis_index("y")
    return lax.axis_index("x"), lax.axis_index("core"), jnp.minimum(column, HEADS - 1)


def attend_kernel(slots, sources, targets, lengths, steps, qd, gain, *refs):
    chunks = refs[0:8]
    dq_hbm, mine_hbm, other_hbm = refs[8:11]
    (kv, kt, q_rows, d_rows, q_cols, d_cols, head_gain, q_ends, weights, d_probs, dkv, dq_cols, dq_rows) = refs[11:24]
    (tops, weight_sums, product_sums, delta, q_sems, kv_sems, out_sems) = refs[24:]
    my_x, my_core, my_head = place()

    def slot_at(zlo, x, core):
        return slots[zlo * (X * CORES) + x * CORES + core]

    def block(index):
        return pl.ds(pl.multiple_of(index * BLK, BLK), BLK)

    mine = [slot_at(b, my_x, my_core) for b in range(ZLO)]
    ranks = []
    for b in range(ZLO):
        rank = jnp.int32(0)
        for other in range(ZLO):
            if other != b:
                rank = rank + (mine[other] < mine[b]).astype(jnp.int32)
        ranks.append(rank)
    ordered = []
    for r in range(ZLO):
        value = jnp.int32(0)
        for b in range(ZLO):
            value = jnp.where(ranks[b] == r, mine[b], value)
        ordered.append(value)

    for i in range(CORES * X):
        pltpu.make_async_copy(
            chunks[i], kv.at[i * QROWS : (i + 1) * QROWS], kv_sems.at[i]
        ).start()

    starts, ends = [], []
    total = jnp.int32(0)
    for s in range(SEGMENTS):
        starts.append(total)
        total = total + lengths[s]
        ends.append(total)

    def end_of(position):
        return sum(jnp.where(starts[s] <= position, lengths[s], 0) for s in range(SEGMENTS))

    def positions(shape, dimension):
        index = lax.broadcasted_iota(jnp.int32, shape, dimension)
        base = jnp.where(index < BLK, ordered[0] * BLK, ordered[1] * BLK - BLK)
        base = jnp.where(index < 2 * BLK, base, ordered[2] * BLK - 2 * BLK)
        base = jnp.where(index < 3 * BLK, base, ordered[3] * BLK - 3 * BLK)
        return base + index

    bounds = []
    for g in range(GROUPS):
        row = (g + 1) * QG - 1
        last = ordered[row // BLK] * BLK + row % BLK
        bounds.append((end_of(last) + TK - 1) // TK)
    whole_tiles = end_of(ordered[0] * BLK) // TK

    def for_tiles(body, split_whole=False):
        for g in range(GROUPS):
            begin = bounds[g - 1] if g else jnp.int32(0)
            lanes = slice(g * QG, QROWS)
            if split_whole and g == 0:
                lax.fori_loop(0, whole_tiles, functools.partial(body, lanes, False), 0)
                begin = whole_tiles
            lax.fori_loop(begin, bounds[g], functools.partial(body, lanes, True), 0)

    q_ends[...] = end_of(positions((1, QROWS), 1))
    tops[...] = jnp.full_like(tops, NEGATIVE)
    weight_sums[...] = jnp.zeros_like(weight_sums)
    product_sums[...] = jnp.zeros_like(product_sums)
    dq_cols[...] = jnp.zeros_like(dq_cols)

    for b in range(ZLO):
        q_rows[block(ranks[b]), :] = qd[b * BLK : (b + 1) * BLK, 0:HD]
        d_rows[block(ranks[b]), :] = qd[b * BLK : (b + 1) * BLK, HD:]
    head_gain[...] = gain[:, pl.ds(pl.multiple_of(my_head * HD, HD), HD)]
    q_cols[...] = q_rows[...].T
    row_positions = positions((QROWS, 1), 0)
    row_gain = jnp.zeros((QROWS, HD), jnp.float32)
    for s in range(SEGMENTS):
        inside = (starts[s] <= row_positions) & (row_positions < ends[s])
        row_gain = jnp.where(inside, head_gain[pl.ds(steps[s], 1), :], row_gain)
    d_rows[...] = (d_rows[...].astype(jnp.float32) * row_gain).astype(jnp.bfloat16)
    d_cols[...] = d_rows[...].T

    def rows_of(t):
        return pl.ds(pl.multiple_of(t * TK, TK), TK)

    def leave(t):
        for i in range(TK // BLK):
            slot = t * (TK // BLK) + i
            target = targets[slot]

            @pl.when(target < X * ZLO)
            def _():
                pltpu.make_async_copy(
                    dkv.at[block(slot)], mine_hbm.at[block(target)], out_sems.at[slot]
                ).start()

            @pl.when(target >= X * ZLO)
            def _():
                pltpu.make_async_copy(
                    dkv.at[block(slot)], other_hbm.at[block(target - X * ZLO)], out_sems.at[slot]
                ).start()

    def total(array):
        return jnp.sum(jnp.sum(array.reshape(-1, 8, array.shape[1]), axis=0), axis=0, keepdims=True)

    def score_tile(lanes, masked, t, carry):
        for part in range(PARTS):
            index = t * PARTS + part
            at = pl.ds(pl.multiple_of(index * TP, TP), TP)
            rows = [block(sources[index * (TP // BLK) + i]) for i in range(TP // BLK)]
            keys = jnp.concatenate([kv[row, 0:HD] for row in rows])
            values = jnp.concatenate([kv[row, HD:] for row in rows])
            kt[:, at] = keys.T
            s = jnp.dot(keys, q_cols[:, lanes], preferred_element_type=jnp.float32)
            dp = jnp.dot(values, d_cols[:, lanes], preferred_element_type=jnp.float32)
            if masked:
                key_position = index * TP + lax.broadcasted_iota(jnp.int32, s.shape, 0)
                s = jnp.where(key_position < q_ends[:, lanes], s, NEGATIVE)
            top = jnp.max(jnp.max(s.reshape(TP // 8, 8, s.shape[1]), axis=0), axis=0, keepdims=True)
            w = jnp.exp2((s - top) * EXP2_SCALE)
            weights[at, lanes] = w
            d_probs[at, lanes] = dp
            row = pl.ds(index, 1)
            tops[row, lanes] = top
            weight_sums[row, lanes] = total(w)
            product_sums[row, lanes] = total(w * dp)
        return carry

    def grad_tile(lanes, masked, t, carry):
        at = rows_of(t)
        probs, shifts = [], []
        for part in range(PARTS):
            index = t * PARTS + part
            here = pl.ds(pl.multiple_of(index * TP, TP), TP)
            p = weights[here, lanes] * weight_sums[pl.ds(index, 1), lanes]
            probs.append(p.astype(jnp.bfloat16))
            shifts.append((p * (d_probs[here, lanes] - delta[:, lanes])).astype(jnp.bfloat16))
        p, shifted = jnp.concatenate(probs), jnp.concatenate(shifts)
        dk = jnp.dot(shifted, q_rows[lanes, :], preferred_element_type=jnp.float32)
        dkv[at, 0:HD] = (dk * SCALING).astype(jnp.bfloat16)
        dv = jnp.dot(p, d_rows[lanes, :], preferred_element_type=jnp.float32)
        dkv[at, HD:] = dv.astype(jnp.bfloat16)
        dq_cols[:, lanes] += jnp.dot(kt[:, at], shifted, preferred_element_type=jnp.float32)
        leave(t)
        return carry

    def unseen_tile(t, carry):
        dkv[rows_of(t), :] = jnp.zeros((TK, 2 * HD), jnp.bfloat16)
        leave(t)
        return carry

    for i in range(CORES * X):
        pltpu.make_async_copy(
            chunks[i], kv.at[i * QROWS : (i + 1) * QROWS], kv_sems.at[i]
        ).wait()
    for_tiles(score_tile, split_whole=True)
    lax.fori_loop(bounds[GROUPS - 1], TOKENS // TK, unseen_tile, 0)
    share = jnp.exp2((tops[...] - jnp.max(tops[...], axis=0, keepdims=True)) * EXP2_SCALE)
    inverse = 1.0 / jnp.sum(weight_sums[...] * share, axis=0, keepdims=True)
    delta[...] = jnp.sum(product_sums[...] * share, axis=0, keepdims=True) * inverse
    weight_sums[...] = share * inverse
    for_tiles(grad_tile)

    dq_rows[...] = (dq_cols[...].T * SCALING).astype(jnp.bfloat16)
    out_copies = [
        pltpu.make_async_copy(dq_rows.at[block(ranks[b])], dq_hbm.at[block(b)], q_sems.at[b])
        for b in range(ZLO)
    ]
    for copy in out_copies:
        copy.start()
    for slot in range(TOKENS // BLK):
        pltpu.make_async_copy(dkv.at[block(slot)], mine_hbm.at[block(0)], out_sems.at[slot]).wait()
    for copy in out_copies:
        copy.wait()


def attend(slots, sources, targets, lengths, steps, qd, gain, chunks):
    smem = pl.BlockSpec(memory_space=pltpu.SMEM)
    hbm = pl.BlockSpec(memory_space=pl.ANY)
    low = jnp.bfloat16
    outs = [
        jax.ShapeDtypeStruct((QROWS, HD), low),
        jax.ShapeDtypeStruct((X * QROWS, 2 * HD), low),
        jax.ShapeDtypeStruct((X * QROWS, 2 * HD), low),
    ]
    return pl.pallas_call(
        attend_kernel,
        out_shape=outs,
        in_specs=[smem] * 5 + [pl.BlockSpec(memory_space=pltpu.VMEM)] * 2 + [hbm] * len(chunks),
        out_specs=[hbm] * len(outs),
        scratch_shapes=[
            pltpu.VMEM((TOKENS, 2 * HD), low),
            pltpu.VMEM((HD, TOKENS), low),
            pltpu.VMEM((QROWS, HD), low),
            pltpu.VMEM((QROWS, HD), low),
            pltpu.VMEM((HD, QROWS), low),
            pltpu.VMEM((HD, QROWS), low),
            pltpu.VMEM((16, HD), jnp.float32),
            pltpu.VMEM((1, QROWS), jnp.int32),
            pltpu.VMEM((TOKENS, QROWS), jnp.float32),
            pltpu.VMEM((TOKENS, QROWS), jnp.float32),
            pltpu.VMEM((TOKENS, 2 * HD), low),
            pltpu.VMEM((HD, QROWS), jnp.float32),
            pltpu.VMEM((QROWS, HD), low),
            pltpu.VMEM((TOKENS // TP, QROWS), jnp.float32),
            pltpu.VMEM((TOKENS // TP, QROWS), jnp.float32),
            pltpu.VMEM((TOKENS // TP, QROWS), jnp.float32),
            pltpu.VMEM((1, QROWS), jnp.float32),
            pltpu.SemaphoreType.DMA((ZLO,)),
            pltpu.SemaphoreType.DMA((CORES * X,)),
            pltpu.SemaphoreType.DMA((TOKENS // BLK,)),
        ],
        compiler_params=pltpu.CompilerParams(vmem_limit_bytes=60 * 1024 * 1024),
    )(slots, sources, targets, lengths, steps, qd, gain, *chunks)


def tables(slots):
    index = jnp.arange(ZLO * X * CORES, dtype=jnp.int32)
    holder = jnp.sum(jnp.where(slots[None, :] == index[:, None], index[None, :], 0), axis=1)
    my_x, my_core, _ = place()
    zlo, x, core = holder // (X * CORES), holder // CORES % X, holder % CORES
    side = (core + my_core) % CORES * X
    return (
        (side + (my_x - x + X) % X) * ZLO + zlo,
        (side + (x - my_x + X) % X) * ZLO + zlo,
    )


def x_shift(array, shift):
    return lax.ppermute(array, "x", [(i, (i + shift) % X) for i in range(X)])


def other_core(array):
    return lax.ppermute(array, "core", [(0, 1), (1, 0)])


def part(array, shift):
    return array[shift * QROWS : (shift + 1) * QROWS]


def by_head(*arrays):
    rows = arrays[0].shape[0]
    parts = [a.reshape(rows, HEADS, HD).transpose(1, 0, 2) for a in arrays]
    joined = jnp.concatenate(parts, axis=2)
    return jnp.pad(joined, ((0, 32 - HEADS), (0, 0), (0, 0)))


def exchange(array):
    return lax.all_to_all(array, COLUMNS, split_axis=0, concat_axis=0, tiled=True)


def by_token(array, rows):
    return array[:HEADS].transpose(1, 0, 2).reshape(rows, HEADS * HD)


def shards(queries, keys, values, d_out, gain, lengths, steps, slots):
    rows = queries.shape[0]
    kv = exchange(by_head(keys, values)).reshape(QROWS, 2 * HD)
    qd = by_head(queries, d_out)
    own = [kv] + [x_shift(kv, s) for s in range(1, X)]
    beside = other_core(kv)
    qd, beside = lax.optimization_barrier((qd, beside))
    qd = exchange(qd).reshape(QROWS, 2 * HD)
    chunks = own + [beside] + [other_core(c) for c in own[1:]]
    dq, mine, other = attend(slots, *tables(slots), lengths, steps, qd, gain, chunks)
    received = other_core(other)
    pair = [
        (part(mine, s).astype(jnp.float32) + part(received, s).astype(jnp.float32)).astype(jnp.bfloat16)
        for s in range(X)
    ]
    total = pair[0].astype(jnp.float32)
    for s in range(1, X):
        total = total + x_shift(pair[s], s).astype(jnp.float32)
    dkv = total.astype(jnp.bfloat16)
    dq = exchange(dq.reshape(32, rows, HD))
    dkv = exchange(dkv.reshape(32, rows, 2 * HD))
    return by_token(dq, rows), by_token(dkv[..., :HD], rows), by_token(dkv[..., HD:], rows)


def solution(mesh):
    split = Mesh(mesh.devices.reshape(ZLO, X, CORES, 2, 4), TOKEN_AXES)
    tokens = P(TOKEN_AXES, None)
    return jax.shard_map(
        shards,
        mesh=split,
        in_specs=(tokens,) * 4 + (P(),) * 4,
        out_specs=(tokens,) * 3,
        check_vma=False,
    )
```

time: 166 us -> 127 us (0.77); the launches traced: 164 us -> 126 us
  Pallas kernels: 44.9 us -> 13.1 us
  waiting for transfers between devices: 51.9 us -> 44.2 us
  other arithmetic: 3.31 us -> 6.45 us
    pallas_call x1, Pallas kernels: 44.9 us -> 13.1 us  [attend(): pl.pallas_call(attend_kernel, out_shape=outs, in_specs=[smem] * 5 + [pl.B...]
    all_to_all x4 -> x3, waiting for transfers between devices: 26.2 us -> 14.8 us  [exchange(): lax.all_to_all(array, COLUMNS, split_axis=0, concat_axis=0, tiled=True)]
    all_to_all x4 -> x3, starting transfers between devices: 18.8 us -> 13 us  [exchange(): lax.all_to_all(array, COLUMNS, split_axis=0, concat_axis=0, tiled=True)]
    ppermute x5, starting transfers between devices: 0.71 us -> 6.37 us  [other_core(): return lax.ppermute(array, 'core', [(0, 1), (1, 0)])]
    ppermute x6, waiting for transfers between devices: 22.1 us -> 25.5 us  [x_shift(): return lax.ppermute(array, 'x', [(i, (i + shift) % X) for i in range(X)])]
  transfers between devices with their start and end apart: 15 -> 14, of which waited for: 7 -> 8; matrix products, arithmetic and copies ran while one was open for 3% -> 4% of each run, Pallas kernels for 0% -> 0%
where the time goes in v2:
time: 127 us; the launch traced here: 126 us
  waiting for transfers between devices  44.2 us (35%)
  starting transfers between devices  30.5 us (24%)
  blocking collectives  26.6 us (21%)
  Pallas kernels  13.1 us (10%)
  other arithmetic  6.45 us (5%)
  local copies, waits for them, and re-layouts  4.75 us (4%)
    all_to_all x1, blocking collectives, exchange(): lax.all_to_all(array, COLUMNS, split_axis=0, concat_axis=0, tiled=True)  26.6 us
    ppermute x6, waiting for transfers between devices, x_shift(): return lax.ppermute(array, 'x', [(i, (i + shift) % X) for i in range(X)])  25.5 us
    all_to_all x3, waiting for transfers between devices, exchange(): lax.all_to_all(array, COLUMNS, split_axis=0, concat_axis=0, tiled=True)  14.8 us
    pallas_call x1, Pallas kernels, attend(): pl.pallas_call(attend_kernel, out_shape=outs, in_specs=[smem] * 5 + [pl.B...  13.1 us
    all_to_all x3, starting transfers between devices, exchange(): lax.all_to_all(array, COLUMNS, split_axis=0, concat_axis=0, tiled=True)  13 us
    ppermute x6, starting transfers between devices, x_shift(): return lax.ppermute(array, 'x', [(i, (i + shift) % X) for i in range(X)])  11.2 us
    ppermute x5, starting transfers between devices, other_core(): return lax.ppermute(array, 'core', [(0, 1), (1, 0)])  6.37 us
    ppermute x5, waiting for transfers between devices, other_core(): return lax.ppermute(array, 'core', [(0, 1), (1, 0)])  3.95 us
  transfers between devices with their start and end apart: 14, of which 8 were waited for; matrix products, arithmetic and copies ran while one was open for 4% of the time, Pallas kernels for 0%

profile of v2, /device:TPU:32, one launch (start us, length us, event | category | flops | bytes accessed | tf_op | source)
XLA Modules:
  0.0 126.4 jit_solution(11967363426023009649)
XLA Ops:
  0.7 0.9 copy-done
  1.5 1.0 bitcast_bitcast_fusion
  2.6 26.6 %all_to_all.20 = bf16[32,24,256]{2,1,0:T(8,128)(2,1)S(1)} all-to-all(bf16[32,24,256]{2,1,0:T(8,128)(2,1)S(1)} %fusion.5), channel_id=1, replica_groups=mesh['zlo'=4,'x'=4,'core'=2,'zhi'=2,'y'=4] {'zlo','zhi','y'}, dimensions={0} | all-to-all | bytes 786432 | tf_op jit(solution)/shard_map/all_to_all | solution.py:289
  29.2 2.8 %collective-permute-start.3 = (bf16[768,256]{1,0:T(8,128)(2,1)S(1)}, bf16[768,256]{1,0:T(8,128)(2,1)S(1)}, u32[]{:S(2)}, u32[]{:S(2)}) collective-permute-start(bf16[768,256]{1,0:T(8,128)(2,1)S(1)} %bitcast.51), channel_id=1, source_target_pairs={{0,48},{16,0},{32,16},{48,32},{1,49},{17,1},{33,17},{49,33},{2,50}... | collective-permute-start | bytes 1179656 | tf_op jit(solution)/shard_map/ppermute | solution.py:270
  32.0 0.8 collective-permute-start.2
  32.8 0.9 collective-permute-start.1
  33.7 0.8 fusion.4
  34.5 4.3 %all-to-all-start.1 = ((bf16[32,24,256]{2,1,0:T(8,128)(2,1)}), bf16[32,24,256]{2,1,0:T(8,128)(2,1)S(1)}, u32[]{:S(2)}, u32[]{:S(2)}) async-start(bf16[32,24,256]{2,1,0:T(8,128)(2,1)} %fusion.4), calls=%async_computation.1 | async-start | bytes 786432 | tf_op jit(solution)/shard_map/all_to_all | solution.py:289
  39.0 10.6 %collective-permute-done.3.refs_3_ = bf16[768,256]{1,0:T(8,128)(2,1)S(1)} collective-permute-done((bf16[768,256]{1,0:T(8,128)(2,1)S(1)}, bf16[768,256]{1,0:T(8,128)(2,1)S(1)}, u32[]{:S(2)}, u32[]{:S(2)}) %collective-permute-start.3) | collective-permute-done | bytes 393248 | tf_op jit(solution)/shard_map/ppermute | solution.py:270
  50.0 3.2 %collective-permute-done.1.refs_1_ = bf16[768,256]{1,0:T(8,128)(2,1)S(1)} collective-permute-done((bf16[768,256]{1,0:T(8,128)(2,1)S(1)}, bf16[768,256]{1,0:T(8,128)(2,1)S(1)}, u32[]{:S(2)}, u32[]{:S(2)}) %collective-permute-start.1) | collective-permute-done | bytes 393248 | tf_op jit(solution)/shard_map/ppermute | solution.py:270
  54.4 0.7 collective-permute-done.4.refs_5_
  55.8 13.1 %shard_map.103 = (bf16[768,128]{1,0:T(8,128)(2,1)}, bf16[3072,256]{1,0:T(8,128)(2,1)}, bf16[3072,256]{1,0:T(8,128)(2,1)}) custom-call(s32[32]{0:T(128)} %slots.1, s32[32]{0:T(128)} %multiply_add_fusion.1.sources, s32[32]{0:T(128)} %get-tuple-element.13.targets, s32[8]{0:T(128)} %lengths.1, s32[8]{0:T(128)} %steps.1, bf16[768,256]{1,0:T(8,128)(2,1)} %bitcast.55, ...), custom_call_target="tpu_custom_call" | custom-call | tf_op jit(solution)/shard_map/pallas_call | solution.py:226
  69.0 5.8 %collective-permute-start.7 = (bf16[3072,256]{1,0:T(8,128)(2,1)}, bf16[3072,256]{1,0:T(8,128)(2,1)S(1)}, u32[]{:S(2)}, u32[]{:S(2)}) collective-permute-start(bf16[3072,256]{1,0:T(8,128)(2,1)} %get-tuple-element.12), channel_id=1, source_target_pairs={{0,8},{8,0},{1,9},{9,1},{2,10},{10,2},{3,11},{11,3},{4,12},{12,4},... | collective-permute-start | bytes 4718600 | tf_op jit(solution)/shard_map/ppermute | solution.py:274
  74.8 3.2 %collective-permute-done.7 = bf16[3072,256]{1,0:T(8,128)(2,1)S(1)} collective-permute-done((bf16[3072,256]{1,0:T(8,128)(2,1)}, bf16[3072,256]{1,0:T(8,128)(2,1)S(1)}, u32[]{:S(2)}, u32[]{:S(2)}) %collective-permute-start.7) | collective-permute-done | bytes 1572896 | tf_op jit(solution)/shard_map/ppermute | solution.py:274
  78.0 2.3 %add_convert_fusion.3 = (bf16[768,256]{1,0:T(8,128)(2,1)}, bf16[768,256]{1,0:T(8,128)(2,1)S(1)}, bf16[768,256]{1,0:T(8,128)(2,1)S(1)}) fusion(bf16[3072,256]{1,0:T(8,128)(2,1)S(1)} %collective-permute-done.7, bf16[3072,256]{1,0:T(8,128)(2,1)} %get-tuple-element.11), kind=kLoop, calls=%fused_computation.8 | loop fusion | flops 2359296 | bytes 3538944 | tf_op jit(solution)/shard_map/convert_element_type | solution.py:308
  80.3 3.2 %collective-permute-start.10 = (bf16[768,256]{1,0:T(8,128)(2,1)S(1)}, bf16[768,256]{1,0:T(8,128)(2,1)S(1)}, u32[]{:S(2)}, u32[]{:S(2)}) collective-permute-start(bf16[768,256]{1,0:T(8,128)(2,1)S(1)} %get-tuple-element.18), channel_id=1, source_target_pairs={{0,48},{16,0},{32,16},{48,32},{1,49},{17,1},{33,17},{49,33},{2,50}... | collective-permute-start | bytes 1179656 | tf_op jit(solution)/shard_map/ppermute | solution.py:270
  83.6 3.4 %collective-permute-start.9 = (bf16[768,256]{1,0:T(8,128)(2,1)S(1)}, bf16[768,256]{1,0:T(8,128)(2,1)}, u32[]{:S(2)}, u32[]{:S(2)}) collective-permute-start(bf16[768,256]{1,0:T(8,128)(2,1)S(1)} %get-tuple-element.19), channel_id=1, source_target_pairs={{0,32},{16,48},{32,0},{48,16},{1,33},{17,49},{33,1},{49,17},{2,34}... | collective-permute-start | bytes 1179656 | tf_op jit(solution)/shard_map/ppermute | solution.py:270
  87.0 4.3 %all-to-all-start.2 = ((bf16[32,24,128]{2,1,0:T(8,128)(2,1)}), bf16[32,24,128]{2,1,0:T(8,128)(2,1)S(1)}, u32[]{:S(2)}, u32[]{:S(2)}) async-start(bf16[32,24,128]{2,1,0:T(8,128)(2,1)} %bitcast.56), calls=%async_computation.2 | async-start | bytes 393216 | tf_op jit(solution)/shard_map/all_to_all | solution.py:289
  91.3 1.8 %collective-permute-done.8 = bf16[768,256]{1,0:T(8,128)(2,1)S(1)} collective-permute-done((bf16[768,256]{1,0:T(8,128)(2,1)}, bf16[768,256]{1,0:T(8,128)(2,1)S(1)}, u32[]{:S(2)}, u32[]{:S(2)}) %collective-permute-start.8) | collective-permute-done | bytes 393248 | tf_op jit(solution)/shard_map/ppermute | solution.py:270
  93.1 1.7 %collective-permute-done.10 = bf16[768,256]{1,0:T(8,128)(2,1)S(1)} collective-permute-done((bf16[768,256]{1,0:T(8,128)(2,1)S(1)}, bf16[768,256]{1,0:T(8,128)(2,1)S(1)}, u32[]{:S(2)}, u32[]{:S(2)}) %collective-permute-start.10) | collective-permute-done | bytes 393248 | tf_op jit(solution)/shard_map/ppermute | solution.py:270
  94.8 8.3 %collective-permute-done.9 = bf16[768,256]{1,0:T(8,128)(2,1)} collective-permute-done((bf16[768,256]{1,0:T(8,128)(2,1)S(1)}, bf16[768,256]{1,0:T(8,128)(2,1)}, u32[]{:S(2)}, u32[]{:S(2)}) %collective-permute-start.9) | collective-permute-done | bytes 393248 | tf_op jit(solution)/shard_map/ppermute | solution.py:270
  103.1 2.1 %add_convert_fusion = bf16[768,256]{1,0:T(8,128)(2,1)} fusion(bf16[768,256]{1,0:T(8,128)(2,1)S(1)} %collective-permute-done.10, bf16[768,256]{1,0:T(8,128)(2,1)} %collective-permute-done.9, bf16[768,256]{1,0:T(8,128)(2,1)S(1)} %collective-permute-done.8, bf16[3072,256]{1,0:T(8,128)(2,1)S(1)} %collective-permute-done.7, bf16[3072,256]{1,0:T(8,128)(2,1)} %get-tuple-element.11), kind=kLoop, calls=%fused_computation.5 | loop fusion | flops 2359296 | bytes 2359296 | tf_op jit(solution)/shard_map/convert_element_type | solution.py:314
  105.2 4.3 %all-to-all-start.3 = ((bf16[32,24,256]{2,1,0:T(8,128)(2,1)}), bf16[32,24,256]{2,1,0:T(8,128)(2,1)S(1)}, u32[]{:S(2)}, u32[]{:S(2)}) async-start(bf16[32,24,256]{2,1,0:T(8,128)(2,1)} %bitcast.8), calls=%async_computation.3 | async-start | bytes 786432 | tf_op jit(solution)/shard_map/all_to_all | solution.py:289
  110.2 14.7 %all-to-all-done.3 = bf16[32,24,256]{2,1,0:T(8,128)(2,1)S(1)} async-done(((bf16[32,24,256]{2,1,0:T(8,128)(2,1)}), bf16[32,24,256]{2,1,0:T(8,128)(2,1)S(1)}, u32[]{:S(2)}, u32[]{:S(2)}) %all-to-all-start.3) | async-done | bytes 393248 | tf_op jit(solution)/shard_map/all_to_all | solution.py:289
  (43 shorter events, 4.7 us)
Async XLA Ops:
  0.6 0.9 copy-start
  0.6 28.5 %copy-start.10 = (bf16[24,3072]{1,0:T(8,128)(2,1)S(1)}, bf16[24,3072]{1,0:T(8,128)(2,1)}, u32[]{:S(2)}) copy-start(bf16[24,3072]{1,0:T(8,128)(2,1)} %param.11) | copy-start | bytes 442372
  0.7 28.5 %copy-start.9 = (bf16[24,3072]{1,0:T(8,128)(2,1)S(1)}, bf16[24,3072]{1,0:T(8,128)(2,1)}, u32[]{:S(2)}) copy-start(bf16[24,3072]{1,0:T(8,128)(2,1)} %param.8) | copy-start | bytes 442372
  2.6 36.3 %copy-start.11 = (s32[32]{0:T(128)S(1)}, s32[32]{0:T(128)}, u32[]{:S(2)}) copy-start(s32[32]{0:T(128)} %slots.1) | copy-start | bytes 388
  29.1 25.9 %copy-start.1 = (bf16[32,24,256]{2,1,0:T(8,128)(2,1)}, bf16[32,24,256]{2,1,0:T(8,128)(2,1)S(1)}, u32[]{:S(2)}) copy-start(bf16[32,24,256]{2,1,0:T(8,128)(2,1)S(1)} %all_to_all.20) | copy-start | bytes 1179652
  29.1 5.4 %collective-permute-start = (bf16[768,256]{1,0:T(8,128)(2,1)S(1)}, bf16[768,256]{1,0:T(8,128)(2,1)S(1)}, u32[]{:S(2)}, u32[]{:S(2)}) collective-permute-start(bf16[768,256]{1,0:T(8,128)(2,1)S(1)} %bitcast.50), channel_id=1, source_target_pairs={{0,8},{8,0},{1,9},{9,1},{2,10},{10,2},{3,11},{11,3},{4,12},{12,4},... | collective-permute-start | bytes 1179656 | tf_op jit(solution)/shard_map/ppermute | solution.py:274
  29.2 20.3 %collective-permute-start.3 = (bf16[768,256]{1,0:T(8,128)(2,1)S(1)}, bf16[768,256]{1,0:T(8,128)(2,1)S(1)}, u32[]{:S(2)}, u32[]{:S(2)}) collective-permute-start(bf16[768,256]{1,0:T(8,128)(2,1)S(1)} %bitcast.51), channel_id=1, source_target_pairs={{0,48},{16,0},{32,16},{48,32},{1,49},{17,1},{33,17},{49,33},{2,50}... | collective-permute-start | bytes 1179656 | tf_op jit(solution)/shard_map/ppermute | solution.py:270
  32.0 17.5 %collective-permute-start.2 = (bf16[768,256]{1,0:T(8,128)(2,1)S(1)}, bf16[768,256]{1,0:T(8,128)(2,1)S(1)}, u32[]{:S(2)}, u32[]{:S(2)}) collective-permute-start(bf16[768,256]{1,0:T(8,128)(2,1)S(1)} %bitcast.52), channel_id=1, source_target_pairs={{0,32},{16,48},{32,0},{48,16},{1,33},{17,49},{33,1},{49,17},{2,34}... | collective-permute-start | bytes 1179656 | tf_op jit(solution)/shard_map/ppermute | solution.py:270
  32.8 20.4 %collective-permute-start.1 = (bf16[768,256]{1,0:T(8,128)(2,1)S(1)}, bf16[768,256]{1,0:T(8,128)(2,1)S(1)}, u32[]{:S(2)}, u32[]{:S(2)}) collective-permute-start(bf16[768,256]{1,0:T(8,128)(2,1)S(1)} %bitcast.53), channel_id=1, source_target_pairs={{0,16},{16,32},{32,48},{48,0},{1,17},{17,33},{33,49},{49,1},{2,18}... | collective-permute-start | bytes 1179656 | tf_op jit(solution)/shard_map/ppermute | solution.py:270
  34.5 20.5 %copy-start.3 = (bf16[768,256]{1,0:T(8,128)(2,1)}, bf16[768,256]{1,0:T(8,128)(2,1)S(1)}, u32[]{:S(2)}) copy-start(bf16[768,256]{1,0:T(8,128)(2,1)S(1)} %collective-permute-done.refs_4_) | copy-start | bytes 1179652
  34.5 20.5 %all-to-all-start.1 = ((bf16[32,24,256]{2,1,0:T(8,128)(2,1)}), bf16[32,24,256]{2,1,0:T(8,128)(2,1)S(1)}, u32[]{:S(2)}, u32[]{:S(2)}) async-start(bf16[32,24,256]{2,1,0:T(8,128)(2,1)} %fusion.4), calls=%async_computation.1 | async-start | bytes 786432 | tf_op jit(solution)/shard_map/all_to_all | solution.py:289
  49.5 5.6 %copy-start.4 = (bf16[768,256]{1,0:T(8,128)(2,1)}, bf16[768,256]{1,0:T(8,128)(2,1)S(1)}, u32[]{:S(2)}) copy-start(bf16[768,256]{1,0:T(8,128)(2,1)S(1)} %collective-permute-done.3.refs_3_) | copy-start | bytes 1179652
  49.5 4.8 %collective-permute-start.6 = (bf16[768,256]{1,0:T(8,128)(2,1)S(1)}, bf16[768,256]{1,0:T(8,128)(2,1)S(1)}, u32[]{:S(2)}, u32[]{:S(2)}) collective-permute-start(bf16[768,256]{1,0:T(8,128)(2,1)S(1)} %collective-permute-done.3.refs_3_), channel_id=1, source_target_pairs={{0,8},{8,0},{1,9},{9,1},{2,10},{10,2},{3,11},{11,3},{4,12},{12,4},... | collective-permute-start | bytes 1179656 | tf_op jit(solution)/shard_map/ppermute | solution.py:274
  49.5 5.6 %copy-start.5 = (bf16[768,256]{1,0:T(8,128)(2,1)}, bf16[768,256]{1,0:T(8,128)(2,1)S(1)}, u32[]{:S(2)}) copy-start(bf16[768,256]{1,0:T(8,128)(2,1)S(1)} %collective-permute-done.2.refs_2_) | copy-start | bytes 1179652
  49.5 4.8 %collective-permute-start.5 = (bf16[768,256]{1,0:T(8,128)(2,1)S(1)}, bf16[768,256]{1,0:T(8,128)(2,1)S(1)}, u32[]{:S(2)}, u32[]{:S(2)}) collective-permute-start(bf16[768,256]{1,0:T(8,128)(2,1)S(1)} %collective-permute-done.2.refs_2_), channel_id=1, source_target_pairs={{0,8},{8,0},{1,9},{9,1},{2,10},{10,2},{3,11},{11,3},{4,12},{12,4},... | collective-permute-start | bytes 1179656 | tf_op jit(solution)/shard_map/ppermute | solution.py:274
  53.2 1.9 %copy-start.6 = (bf16[768,256]{1,0:T(8,128)(2,1)}, bf16[768,256]{1,0:T(8,128)(2,1)S(1)}, u32[]{:S(2)}) copy-start(bf16[768,256]{1,0:T(8,128)(2,1)S(1)} %collective-permute-done.1.refs_1_) | copy-start | bytes 1179652
  53.2 1.9 %collective-permute-start.4 = (bf16[768,256]{1,0:T(8,128)(2,1)S(1)}, bf16[768,256]{1,0:T(8,128)(2,1)}, u32[]{:S(2)}, u32[]{:S(2)}) collective-permute-start(bf16[768,256]{1,0:T(8,128)(2,1)S(1)} %collective-permute-done.1.refs_1_), channel_id=1, source_target_pairs={{0,8},{8,0},{1,9},{9,1},{2,10},{10,2},{3,11},{11,3},{4,12},{12,4},... | collective-permute-start | bytes 1179656 | tf_op jit(solution)/shard_map/ppermute | solution.py:274
  54.4 0.9 copy-start.8
  69.0 9.1 %collective-permute-start.7 = (bf16[3072,256]{1,0:T(8,128)(2,1)}, bf16[3072,256]{1,0:T(8,128)(2,1)S(1)}, u32[]{:S(2)}, u32[]{:S(2)}) collective-permute-start(bf16[3072,256]{1,0:T(8,128)(2,1)} %get-tuple-element.12), channel_id=1, source_target_pairs={{0,8},{8,0},{1,9},{9,1},{2,10},{10,2},{3,11},{11,3},{4,12},{12,4},... | collective-permute-start | bytes 4718600 | tf_op jit(solution)/shard_map/ppermute | solution.py:274
  80.3 12.8 %collective-permute-start.8 = (bf16[768,256]{1,0:T(8,128)(2,1)}, bf16[768,256]{1,0:T(8,128)(2,1)S(1)}, u32[]{:S(2)}, u32[]{:S(2)}) collective-permute-start(bf16[768,256]{1,0:T(8,128)(2,1)} %get-tuple-element.17), channel_id=1, source_target_pairs={{0,16},{16,32},{32,48},{48,0},{1,17},{17,33},{33,49},{49,1},{2,18}... | collective-permute-start | bytes 1179656 | tf_op jit(solution)/shard_map/ppermute | solution.py:270
  80.3 14.5 %collective-permute-start.10 = (bf16[768,256]{1,0:T(8,128)(2,1)S(1)}, bf16[768,256]{1,0:T(8,128)(2,1)S(1)}, u32[]{:S(2)}, u32[]{:S(2)}) collective-permute-start(bf16[768,256]{1,0:T(8,128)(2,1)S(1)} %get-tuple-element.18), channel_id=1, source_target_pairs={{0,48},{16,0},{32,16},{48,32},{1,49},{17,1},{33,17},{49,33},{2,50}... | collective-permute-start | bytes 1179656 | tf_op jit(solution)/shard_map/ppermute | solution.py:270
  83.6 19.5 %collective-permute-start.9 = (bf16[768,256]{1,0:T(8,128)(2,1)S(1)}, bf16[768,256]{1,0:T(8,128)(2,1)}, u32[]{:S(2)}, u32[]{:S(2)}) collective-permute-start(bf16[768,256]{1,0:T(8,128)(2,1)S(1)} %get-tuple-element.19), channel_id=1, source_target_pairs={{0,32},{16,48},{32,0},{48,16},{1,33},{17,49},{33,1},{49,17},{2,34}... | collective-permute-start | bytes 1179656 | tf_op jit(solution)/shard_map/ppermute | solution.py:270
  87.0 18.3 %all-to-all-start.2 = ((bf16[32,24,128]{2,1,0:T(8,128)(2,1)}), bf16[32,24,128]{2,1,0:T(8,128)(2,1)S(1)}, u32[]{:S(2)}, u32[]{:S(2)}) async-start(bf16[32,24,128]{2,1,0:T(8,128)(2,1)} %bitcast.56), calls=%async_computation.2 | async-start | bytes 393216 | tf_op jit(solution)/shard_map/all_to_all | solution.py:289
  105.2 19.8 %all-to-all-start.3 = ((bf16[32,24,256]{2,1,0:T(8,128)(2,1)}), bf16[32,24,256]{2,1,0:T(8,128)(2,1)S(1)}, u32[]{:S(2)}, u32[]{:S(2)}) async-start(bf16[32,24,256]{2,1,0:T(8,128)(2,1)} %bitcast.8), calls=%async_computation.3 | async-start | bytes 786432 | tf_op jit(solution)/shard_map/all_to_all | solution.py:289
  (2 other events, 1.5 us)

commit v3 on v2

--- a/solution.py
+++ b/solution.py
@@ -18,12 +18,15 @@
 QG = 384
 GROUPS = QROWS // QG
 TK = 768
+SCORE_UNROLL = 2
+GRAD_UNROLL = 2
 PARTS = 2
 TP = TK // PARTS
 X = 4
 ZLO = 4
 CORES = 2
 NEGATIVE = -1e30
+SENT = (1, 3, 2, 0)
 SCALING = 1.0 / math.sqrt(HD)
 EXP2_SCALE = SCALING * math.log2(math.e)
 COLUMNS = ("zlo", "zhi", "y")
@@ -35,11 +38,11 @@
     return lax.axis_index("x"), lax.axis_index("core"), jnp.minimum(column, HEADS - 1)
 
 
-def attend_kernel(slots, sources, targets, lengths, steps, qd, gain, *refs):
+def attend_kernel(slots, lengths, steps, qd, gain, *refs):
     chunks = refs[0:8]
-    dq_hbm, mine_hbm, other_hbm = refs[8:11]
-    (kv, kt, q_rows, d_rows, q_cols, d_cols, head_gain, q_ends, weights, d_probs, dkv, dq_cols, dq_rows) = refs[11:24]
-    (tops, weight_sums, product_sums, delta, q_sems, kv_sems, out_sems) = refs[24:]
+    dq_hbm, mine_hbm, near_hbm, far_hbm = refs[8:12]
+    (kv, kt, q_rows, d_rows, q_cols, d_cols, head_gain, spans, weights, d_probs, dkv, dq_cols, dq_rows) = refs[12:25]
+    (tops, weight_sums, product_sums, delta, sources, targets, q_sems, kv_sems, out_sems) = refs[25:]
     my_x, my_core, my_head = place()
 
     def slot_at(zlo, x, core):
@@ -68,6 +71,14 @@
             chunks[i], kv.at[i * QROWS : (i + 1) * QROWS], kv_sems.at[i]
         ).start()
 
+    for c in range(CORES):
+        for s in range(X):
+            for b in range(ZLO):
+                x = (my_x + s) % X
+                core = (my_core + c) % CORES
+                targets[slot_at(b, x, core)] = (c * X + SENT.index(s)) * ZLO + b
+                sources[slot_at(b, x, core)] = (c * X + (X - s) % X) * ZLO + b
+
     starts, ends = [], []
     total = jnp.int32(0)
     for s in range(SEGMENTS):
@@ -90,18 +101,39 @@
         row = (g + 1) * QG - 1
         last = ordered[row // BLK] * BLK + row % BLK
         bounds.append((end_of(last) + TK - 1) // TK)
-    whole_tiles = end_of(ordered[0] * BLK) // TK
-
-    def for_tiles(body, split_whole=False):
+
+    def for_tiles(body, unroll):
         for g in range(GROUPS):
-            begin = bounds[g - 1] if g else jnp.int32(0)
+            begin, end = bounds[g - 1] if g else jnp.int32(0), bounds[g]
             lanes = slice(g * QG, QROWS)
-            if split_whole and g == 0:
-                lax.fori_loop(0, whole_tiles, functools.partial(body, lanes, False), 0)
-                begin = whole_tiles
-            lax.fori_loop(begin, bounds[g], functools.partial(body, lanes, True), 0)
-
-    q_ends[...] = end_of(positions((1, QROWS), 1))
+            runs = 0
+            if unroll > 1:
+                runs = jnp.maximum(end - begin, 0) // unroll
+                lax.fori_loop(
+                    0, runs, lambda i, c: body(lanes, unroll, begin + i * unroll, c), 0
+                )
+            lax.fori_loop(begin + runs * unroll, end, functools.partial(body, lanes, 1), 0)
+
+    span = lax.broadcasted_iota(jnp.int32, (HD, 1), 0)
+    q_end = end_of(positions((1, QROWS), 1))
+    hidden = jnp.zeros((HD, QROWS), jnp.float32)
+    lane = lax.broadcasted_iota(jnp.int32, (1, HD), 1)
+    low, high = jnp.full((1, HD), TOKENS, jnp.int32), jnp.zeros((1, HD), jnp.int32)
+    for s in range(SEGMENTS):
+        hidden = jnp.where((span == s) & (starts[s] >= q_end), NEGATIVE, hidden)
+        low, high = jnp.where(lane == s, starts[s], low), jnp.where(lane == s, ends[s], high)
+    q_cols[HD:, :] = hidden.astype(jnp.bfloat16)
+
+    def mark_tile(t, carry):
+        key_position = t * TK + lax.broadcasted_iota(jnp.int32, (TK, HD), 0)
+        inside = (low <= key_position) & (key_position < high)
+        spans[rows_of(t), :] = jnp.where(inside, 1.0, 0.0).astype(jnp.bfloat16)
+        return carry
+
+    def rows_of(t, count=1):
+        return pl.ds(pl.multiple_of(t * TK, TK), count * TK)
+
+    lax.fori_loop(0, bounds[GROUPS - 1], mark_tile, 0)
     tops[...] = jnp.full_like(tops, NEGATIVE)
     weight_sums[...] = jnp.zeros_like(weight_sums)
     product_sums[...] = jnp.zeros_like(product_sums)
@@ -111,7 +143,7 @@
         q_rows[block(ranks[b]), :] = qd[b * BLK : (b + 1) * BLK, 0:HD]
         d_rows[block(ranks[b]), :] = qd[b * BLK : (b + 1) * BLK, HD:]
     head_gain[...] = gain[:, pl.ds(pl.multiple_of(my_head * HD, HD), HD)]
-    q_cols[...] = q_rows[...].T
+    q_cols[0:HD, :] = q_rows[...].T
     row_positions = positions((QROWS, 1), 0)
     row_gain = jnp.zeros((QROWS, HD), jnp.float32)
     for s in range(SEGMENTS):
@@ -120,9 +152,6 @@
     d_rows[...] = (d_rows[...].astype(jnp.float32) * row_gain).astype(jnp.bfloat16)
     d_cols[...] = d_rows[...].T
 
-    def rows_of(t):
-        return pl.ds(pl.multiple_of(t * TK, TK), TK)
-
     def leave(t):
         for i in range(TK // BLK):
             slot = t * (TK // BLK) + i
@@ -134,28 +163,32 @@
                     dkv.at[block(slot)], mine_hbm.at[block(target)], out_sems.at[slot]
                 ).start()
 
-            @pl.when(target >= X * ZLO)
+            @pl.when((target >= X * ZLO) & (target < (X + 2) * ZLO))
             def _():
                 pltpu.make_async_copy(
-                    dkv.at[block(slot)], other_hbm.at[block(target - X * ZLO)], out_sems.at[slot]
+                    dkv.at[block(slot)], near_hbm.at[block(target - X * ZLO)], out_sems.at[slot]
+                ).start()
+
+            @pl.when(target >= (X + 2) * ZLO)
+            def _():
+                pltpu.make_async_copy(
+                    dkv.at[block(slot)], far_hbm.at[block(target - (X + 2) * ZLO)], out_sems.at[slot]
                 ).start()
 
     def total(array):
         return jnp.sum(jnp.sum(array.reshape(-1, 8, array.shape[1]), axis=0), axis=0, keepdims=True)
 
-    def score_tile(lanes, masked, t, carry):
-        for part in range(PARTS):
+    def score_tile(lanes, count, t, carry):
+        for part in range(count * PARTS):
             index = t * PARTS + part
             at = pl.ds(pl.multiple_of(index * TP, TP), TP)
             rows = [block(sources[index * (TP // BLK) + i]) for i in range(TP // BLK)]
             keys = jnp.concatenate([kv[row, 0:HD] for row in rows])
             values = jnp.concatenate([kv[row, HD:] for row in rows])
             kt[:, at] = keys.T
-            s = jnp.dot(keys, q_cols[:, lanes], preferred_element_type=jnp.float32)
+            marked = jnp.concatenate([keys, spans[at, :]], axis=1)
+            s = jnp.dot(marked, q_cols[:, lanes], preferred_element_type=jnp.float32)
             dp = jnp.dot(values, d_cols[:, lanes], preferred_element_type=jnp.float32)
-            if masked:
-                key_position = index * TP + lax.broadcasted_iota(jnp.int32, s.shape, 0)
-                s = jnp.where(key_position < q_ends[:, lanes], s, NEGATIVE)
             top = jnp.max(jnp.max(s.reshape(TP // 8, 8, s.shape[1]), axis=0), axis=0, keepdims=True)
             w = jnp.exp2((s - top) * EXP2_SCALE)
             weights[at, lanes] = w
@@ -166,10 +199,10 @@
             product_sums[row, lanes] = total(w * dp)
         return carry
 
-    def grad_tile(lanes, masked, t, carry):
-        at = rows_of(t)
+    def grad_tile(lanes, count, t, carry):
+        at = rows_of(t, count)
         probs, shifts = [], []
-        for part in range(PARTS):
+        for part in range(count * PARTS):
             index = t * PARTS + part
             here = pl.ds(pl.multiple_of(index * TP, TP), TP)
             p = weights[here, lanes] * weight_sums[pl.ds(index, 1), lanes]
@@ -181,7 +214,8 @@
         dv = jnp.dot(p, d_rows[lanes, :], preferred_element_type=jnp.float32)
         dkv[at, HD:] = dv.astype(jnp.bfloat16)
         dq_cols[:, lanes] += jnp.dot(kt[:, at], shifted, preferred_element_type=jnp.float32)
-        leave(t)
+        for i in range(count):
+            leave(t + i)
         return carry
 
     def unseen_tile(t, carry):
@@ -193,13 +227,13 @@
         pltpu.make_async_copy(
             chunks[i], kv.at[i * QROWS : (i + 1) * QROWS], kv_sems.at[i]
         ).wait()
-    for_tiles(score_tile, split_whole=True)
+    for_tiles(score_tile, SCORE_UNROLL)
     lax.fori_loop(bounds[GROUPS - 1], TOKENS // TK, unseen_tile, 0)
     share = jnp.exp2((tops[...] - jnp.max(tops[...], axis=0, keepdims=True)) * EXP2_SCALE)
     inverse = 1.0 / jnp.sum(weight_sums[...] * share, axis=0, keepdims=True)
     delta[...] = jnp.sum(product_sums[...] * share, axis=0, keepdims=True) * inverse
     weight_sums[...] = share * inverse
-    for_tiles(grad_tile)
+    for_tiles(grad_tile, GRAD_UNROLL)
 
     dq_rows[...] = (dq_cols[...].T * SCALING).astype(jnp.bfloat16)
     out_copies = [
@@ -214,29 +248,30 @@
         copy.wait()
 
 
-def attend(slots, sources, targets, lengths, steps, qd, gain, chunks):
+def attend(slots, lengths, steps, qd, gain, chunks):
     smem = pl.BlockSpec(memory_space=pltpu.SMEM)
     hbm = pl.BlockSpec(memory_space=pl.ANY)
     low = jnp.bfloat16
     outs = [
         jax.ShapeDtypeStruct((QROWS, HD), low),
         jax.ShapeDtypeStruct((X * QROWS, 2 * HD), low),
-        jax.ShapeDtypeStruct((X * QROWS, 2 * HD), low),
+        jax.ShapeDtypeStruct((2 * QROWS, 2 * HD), low),
+        jax.ShapeDtypeStruct((2 * QROWS, 2 * HD), low),
     ]
     return pl.pallas_call(
         attend_kernel,
         out_shape=outs,
-        in_specs=[smem] * 5 + [pl.BlockSpec(memory_space=pltpu.VMEM)] * 2 + [hbm] * len(chunks),
+        in_specs=[smem] * 3 + [pl.BlockSpec(memory_space=pltpu.VMEM)] * 2 + [hbm] * len(chunks),
         out_specs=[hbm] * len(outs),
         scratch_shapes=[
             pltpu.VMEM((TOKENS, 2 * HD), low),
             pltpu.VMEM((HD, TOKENS), low),
             pltpu.VMEM((QROWS, HD), low),
             pltpu.VMEM((QROWS, HD), low),
-            pltpu.VMEM((HD, QROWS), low),
+            pltpu.VMEM((2 * HD, QROWS), low),
             pltpu.VMEM((HD, QROWS), low),
             pltpu.VMEM((16, HD), jnp.float32),
-            pltpu.VMEM((1, QROWS), jnp.int32),
+            pltpu.VMEM((TOKENS, HD), low),
             pltpu.VMEM((TOKENS, QROWS), jnp.float32),
             pltpu.VMEM((TOKENS, QROWS), jnp.float32),
             pltpu.VMEM((TOKENS, 2 * HD), low),
@@ -246,24 +281,14 @@
             pltpu.VMEM((TOKENS // TP, QROWS), jnp.float32),
             pltpu.VMEM((TOKENS // TP, QROWS), jnp.float32),
             pltpu.VMEM((1, QROWS), jnp.float32),
+            pltpu.SMEM((TOKENS // BLK,), jnp.int32),
+            pltpu.SMEM((TOKENS // BLK,), jnp.int32),
             pltpu.SemaphoreType.DMA((ZLO,)),
             pltpu.SemaphoreType.DMA((CORES * X,)),
             pltpu.SemaphoreType.DMA((TOKENS // BLK,)),
         ],
         compiler_params=pltpu.CompilerParams(vmem_limit_bytes=60 * 1024 * 1024),
-    )(slots, sources, targets, lengths, steps, qd, gain, *chunks)
-
-
-def tables(slots):
-    index = jnp.arange(ZLO * X * CORES, dtype=jnp.int32)
-    holder = jnp.sum(jnp.where(slots[None, :] == index[:, None], index[None, :], 0), axis=1)
-    my_x, my_core, _ = place()
-    zlo, x, core = holder // (X * CORES), holder // CORES % X, holder % CORES
-    side = (core + my_core) % CORES * X
-    return (
-        (side + (my_x - x + X) % X) * ZLO + zlo,
-        (side + (x - my_x + X) % X) * ZLO + zlo,
-    )
+    )(slots, lengths, steps, qd, gain, *chunks)
 
 
 def x_shift(array, shift):
@@ -275,7 +300,8 @@
 
 
 def part(array, shift):
-    return array[shift * QROWS : (shift + 1) * QROWS]
+    at = SENT.index(shift) * QROWS % array.shape[0]
+    return array[at : at + QROWS]
 
 
 def by_head(*arrays):
@@ -296,21 +322,25 @@
 def shards(queries, keys, values, d_out, gain, lengths, steps, slots):
     rows = queries.shape[0]
     kv = exchange(by_head(keys, values)).reshape(QROWS, 2 * HD)
-    qd = by_head(queries, d_out)
-    own = [kv] + [x_shift(kv, s) for s in range(1, X)]
     beside = other_core(kv)
-    qd, beside = lax.optimization_barrier((qd, beside))
-    qd = exchange(qd).reshape(QROWS, 2 * HD)
+    near = {s: x_shift(kv, s) for s in (1, 3)}
+    later, queries, d_out, beside = lax.optimization_barrier((kv, queries, d_out, beside))
+    own = [kv, near[1], x_shift(later, 2), near[3]]
+    qd = exchange(by_head(queries, d_out)).reshape(QROWS, 2 * HD)
     chunks = own + [beside] + [other_core(c) for c in own[1:]]
-    dq, mine, other = attend(slots, *tables(slots), lengths, steps, qd, gain, chunks)
-    received = other_core(other)
-    pair = [
-        (part(mine, s).astype(jnp.float32) + part(received, s).astype(jnp.float32)).astype(jnp.bfloat16)
-        for s in range(X)
-    ]
-    total = pair[0].astype(jnp.float32)
-    for s in range(1, X):
-        total = total + x_shift(pair[s], s).astype(jnp.float32)
+    dq, mine, other_near, other_far = attend(slots, lengths, steps, qd, gain, chunks)
+    received_near, received_far = other_core(other_near), other_core(other_far)
+
+    def pair(shift, received):
+        return part(mine, shift).astype(jnp.float32) + part(received, shift).astype(jnp.float32)
+
+    pairs = [pair(s, received_near).astype(jnp.bfloat16) for s in SENT[:2]]
+    arrived = [x_shift(p, s) for p, s in zip(pairs, SENT)]
+    received_far, *_ = lax.optimization_barrier((received_far, *pairs))
+    arrived.append(x_shift(pair(2, received_far).astype(jnp.bfloat16), 2))
+    total = pair(0, received_far)
+    for array in arrived:
+        total = total + array.astype(jnp.float32)
     dkv = total.astype(jnp.bfloat16)
     dq = exchange(dq.reshape(32, rows, HD))
     dkv = exchange(dkv.reshape(32, rows, 2 * HD))

time: 127 us -> 123 us (0.969)
  starting transfers between devices: 30.5 us -> 24.3 us
  Pallas kernels: 13.1 us -> 15.8 us
    ppermute x5 -> x6, starting transfers between devices: 6.37 us -> 1.09 us  [other_core(): return lax.ppermute(array, 'core', [(0, 1), (1, 0)])]
    pallas_call x1, Pallas kernels: 13.1 us -> 15.8 us  [attend(): pl.pallas_call(attend_kernel, out_shape=outs, in_specs=[smem] * 3 + [pl.B...]
    ppermute x5 -> x6, waiting for transfers between devices: 3.95 us -> 3.53 us  [other_core(): return lax.ppermute(array, 'core', [(0, 1), (1, 0)])]
  transfers between devices with their start and end apart: 14 -> 15, of which waited for: 8 -> 10; matrix products, arithmetic and copies ran while one was open for 4% -> 4% of each run, Pallas kernels for 0% -> 0%
where the time goes in v3:
time: 123 us; the launch traced here: 121 us
  waiting for transfers between devices  44.3 us (36%)
  blocking collectives  26.6 us (22%)
  starting transfers between devices  24.3 us (20%)
  Pallas kernels  15.8 us (13%)
  other arithmetic  5.19 us (4%)
  local copies, waits for them, and re-layouts  4.49 us (4%)
    all_to_all x1, blocking collectives, exchange(): lax.all_to_all(array, COLUMNS, split_axis=0, concat_axis=0, tiled=True)  26.6 us
    ppermute x6, waiting for transfers between devices, x_shift(): return lax.ppermute(array, 'x', [(i, (i + shift) % X) for i in range(X)])  25.3 us
    pallas_call x1, Pallas kernels, attend(): pl.pallas_call(attend_kernel, out_shape=outs, in_specs=[smem] * 3 + [pl.B...  15.8 us
    all_to_all x3, waiting for transfers between devices, exchange(): lax.all_to_all(array, COLUMNS, split_axis=0, concat_axis=0, tiled=True)  15.4 us
    all_to_all x3, starting transfers between devices, exchange(): lax.all_to_all(array, COLUMNS, split_axis=0, concat_axis=0, tiled=True)  13 us
    ppermute x6, starting transfers between devices, x_shift(): return lax.ppermute(array, 'x', [(i, (i + shift) % X) for i in range(X)])  10.2 us
    ppermute x6, waiting for transfers between devices, other_core(): return lax.ppermute(array, 'core', [(0, 1), (1, 0)])  3.53 us
  transfers between devices with their start and end apart: 15, of which 10 were waited for; matrix products, arithmetic and copies ran while one was open for 4% of the time, Pallas kernels for 0%

profile of v3, /device:TPU:32, one launch (start us, length us, event | category | flops | bytes accessed | tf_op | source)
XLA Modules:
  0.0 121.4 jit_solution(1449496335120765783)
XLA Ops:
  0.7 1.0 copy-done
  1.6 1.0 bitcast_bitcast_fusion.2
  2.6 26.6 %all_to_all.20 = bf16[32,24,256]{2,1,0:T(8,128)(2,1)S(1)} all-to-all(bf16[32,24,256]{2,1,0:T(8,128)(2,1)S(1)} %fusion.5), channel_id=1, replica_groups=mesh['zlo'=4,'x'=4,'core'=2,'zhi'=2,'y'=4] {'zlo','zhi','y'}, dimensions={0} | all-to-all | bytes 786432 | tf_op jit(solution)/shard_map/all_to_all | solution.py:315
  29.2 2.8 %collective-permute-start.3 = (bf16[768,256]{1,0:T(8,128)(2,1)S(1)}, bf16[768,256]{1,0:T(8,128)(2,1)S(1)}, u32[]{:S(2)}, u32[]{:S(2)}) collective-permute-start(bf16[768,256]{1,0:T(8,128)(2,1)S(1)} %bitcast.51), channel_id=1, source_target_pairs={{0,48},{16,0},{32,16},{48,32},{1,49},{17,1},{33,17},{49,33},{2,50}... | collective-permute-start | bytes 1179656 | tf_op jit(solution)/shard_map/ppermute | solution.py:295
  32.0 2.4 %collective-permute-start.2 = (bf16[768,256]{1,0:T(8,128)(2,1)S(1)}, bf16[768,256]{1,0:T(8,128)(2,1)S(1)}, u32[]{:S(2)}, u32[]{:S(2)}) collective-permute-start(bf16[768,256]{1,0:T(8,128)(2,1)S(1)} %bitcast.53), channel_id=1, source_target_pairs={{0,32},{16,48},{32,0},{48,16},{1,33},{17,49},{33,1},{49,17},{2,34}... | collective-permute-start | bytes 1179656 | tf_op jit(solution)/shard_map/ppermute | solution.py:295
  34.4 0.8 fusion.4
  35.2 4.3 %all-to-all-start.1 = ((bf16[32,24,256]{2,1,0:T(8,128)(2,1)}), bf16[32,24,256]{2,1,0:T(8,128)(2,1)S(1)}, u32[]{:S(2)}, u32[]{:S(2)}) async-start(bf16[32,24,256]{2,1,0:T(8,128)(2,1)} %fusion.4), calls=%async_computation.1 | async-start | bytes 786432 | tf_op jit(solution)/shard_map/all_to_all | solution.py:315
  39.5 9.9 %collective-permute-done.3.refs_3_ = bf16[768,256]{1,0:T(8,128)(2,1)S(1)} collective-permute-done((bf16[768,256]{1,0:T(8,128)(2,1)S(1)}, bf16[768,256]{1,0:T(8,128)(2,1)S(1)}, u32[]{:S(2)}, u32[]{:S(2)}) %collective-permute-start.3) | collective-permute-done | bytes 393248 | tf_op jit(solution)/shard_map/ppermute | solution.py:295
  49.5 3.4 %collective-permute-done.1.refs_1_ = bf16[768,256]{1,0:T(8,128)(2,1)S(1)} collective-permute-done((bf16[768,256]{1,0:T(8,128)(2,1)S(1)}, bf16[768,256]{1,0:T(8,128)(2,1)S(1)}, u32[]{:S(2)}, u32[]{:S(2)}) %collective-permute-start.1) | collective-permute-done | bytes 393248 | tf_op jit(solution)/shard_map/ppermute | solution.py:295
  53.4 1.2 collective-permute-done.4.refs_5_
  55.7 15.8 %shard_map.103 = (bf16[768,128]{1,0:T(8,128)(2,1)}, bf16[3072,256]{1,0:T(8,128)(2,1)}, bf16[1536,256]{1,0:T(8,128)(2,1)}, bf16[1536,256]{1,0:T(8,128)(2,1)}) custom-call(s32[32]{0:T(128)} %slots.1, s32[8]{0:T(128)} %lengths.1, s32[8]{0:T(128)} %steps.1, bf16[768,256]{1,0:T(8,128)(2,1)} %bitcast.55, f32[16,3072]{1,0:T(8,128)} %gain.1, ...), custom_call_target="tpu_custom_call" | custom-call | tf_op jit(solution)/shard_map/pallas_call | solution.py:261
  72.1 2.0 %collective-permute-done.8 = bf16[1536,256]{1,0:T(8,128)(2,1)S(1)} collective-permute-done((bf16[1536,256]{1,0:T(8,128)(2,1)}, bf16[1536,256]{1,0:T(8,128)(2,1)S(1)}, u32[]{:S(2)}, u32[]{:S(2)}) %collective-permute-start.8) | collective-permute-done | bytes 786464 | tf_op jit(solution)/shard_map/ppermute | solution.py:299
  74.1 1.3 %add_convert_fusion.2 = (bf16[768,256]{1,0:T(8,128)(2,1)S(1)}, bf16[768,256]{1,0:T(8,128)(2,1)S(1)}) fusion(bf16[1536,256]{1,0:T(8,128)(2,1)S(1)} %collective-permute-done.8, bf16[3072,256]{1,0:T(8,128)(2,1)} %get-tuple-element.17), kind=kLoop, calls=%fused_computation.7 | loop fusion | flops 1572864 | bytes 2359296 | tf_op jit(solution)/shard_map/convert_element_type | solution.py:337
  75.4 0.8 add_convert_fusion.1
  76.3 3.1 %collective-permute-start.11 = (bf16[768,256]{1,0:T(8,128)(2,1)}, bf16[768,256]{1,0:T(8,128)(2,1)}, u32[]{:S(2)}, u32[]{:S(2)}) collective-permute-start(bf16[768,256]{1,0:T(8,128)(2,1)} %add_convert_fusion.1), channel_id=1, source_target_pairs={{0,32},{16,48},{32,0},{48,16},{1,33},{17,49},{33,1},{49,17},{2,34}... | collective-permute-start | bytes 1179656 | tf_op jit(solution)/shard_map/ppermute | solution.py:295
  79.3 1.4 %collective-permute-start.10 = (bf16[768,256]{1,0:T(8,128)(2,1)S(1)}, bf16[768,256]{1,0:T(8,128)(2,1)}, u32[]{:S(2)}, u32[]{:S(2)}) collective-permute-start(bf16[768,256]{1,0:T(8,128)(2,1)S(1)} %get-tuple-element.21), channel_id=1, source_target_pairs={{0,48},{16,0},{32,16},{48,32},{1,49},{17,1},{33,17},{49,33},{2,50}... | collective-permute-start | bytes 1179656 | tf_op jit(solution)/shard_map/ppermute | solution.py:295
  81.4 4.3 %all-to-all-start.2 = ((bf16[32,24,128]{2,1,0:T(8,128)(2,1)}), bf16[32,24,128]{2,1,0:T(8,128)(2,1)S(1)}, u32[]{:S(2)}, u32[]{:S(2)}) async-start(bf16[32,24,128]{2,1,0:T(8,128)(2,1)} %bitcast.56), calls=%async_computation.2 | async-start | bytes 393216 | tf_op jit(solution)/shard_map/all_to_all | solution.py:315
  85.7 4.4 %collective-permute-done.11 = bf16[768,256]{1,0:T(8,128)(2,1)} collective-permute-done((bf16[768,256]{1,0:T(8,128)(2,1)}, bf16[768,256]{1,0:T(8,128)(2,1)}, u32[]{:S(2)}, u32[]{:S(2)}) %collective-permute-start.11) | collective-permute-done | bytes 393248 | tf_op jit(solution)/shard_map/ppermute | solution.py:295
  90.1 6.2 %collective-permute-done.10 = bf16[768,256]{1,0:T(8,128)(2,1)} collective-permute-done((bf16[768,256]{1,0:T(8,128)(2,1)S(1)}, bf16[768,256]{1,0:T(8,128)(2,1)}, u32[]{:S(2)}, u32[]{:S(2)}) %collective-permute-start.10) | collective-permute-done | bytes 393248 | tf_op jit(solution)/shard_map/ppermute | solution.py:295
  96.2 1.4 %collective-permute-done.9 = bf16[768,256]{1,0:T(8,128)(2,1)} collective-permute-done((bf16[768,256]{1,0:T(8,128)(2,1)S(1)}, bf16[768,256]{1,0:T(8,128)(2,1)}, u32[]{:S(2)}, u32[]{:S(2)}) %collective-permute-start.9) | collective-permute-done | bytes 393248 | tf_op jit(solution)/shard_map/ppermute | solution.py:295
  97.7 2.2 %add_convert_fusion = bf16[768,256]{1,0:T(8,128)(2,1)} fusion(bf16[768,256]{1,0:T(8,128)(2,1)} %collective-permute-done.11, bf16[768,256]{1,0:T(8,128)(2,1)} %collective-permute-done.10, bf16[768,256]{1,0:T(8,128)(2,1)} %collective-permute-done.9, bf16[1536,256]{1,0:T(8,128)(2,1)S(1)} %collective-permute-done.7, bf16[3072,256]{1,0:T(8,128)(2,1)S(1)} %copy-done.3), kind=kLoop, calls=%fused_computation.5 | loop fusion | flops 1966080 | bytes 2359296 | tf_op jit(solution)/shard_map/convert_element_type | solution.py:344
  99.9 4.3 %all-to-all-start.3 = ((bf16[32,24,256]{2,1,0:T(8,128)(2,1)}), bf16[32,24,256]{2,1,0:T(8,128)(2,1)S(1)}, u32[]{:S(2)}, u32[]{:S(2)}) async-start(bf16[32,24,256]{2,1,0:T(8,128)(2,1)} %bitcast.8), calls=%async_computation.3 | async-start | bytes 786432 | tf_op jit(solution)/shard_map/all_to_all | solution.py:315
  104.9 15.1 %all-to-all-done.3 = bf16[32,24,256]{2,1,0:T(8,128)(2,1)S(1)} async-done(((bf16[32,24,256]{2,1,0:T(8,128)(2,1)}), bf16[32,24,256]{2,1,0:T(8,128)(2,1)S(1)}, u32[]{:S(2)}, u32[]{:S(2)}) %all-to-all-start.3) | async-done | bytes 393248 | tf_op jit(solution)/shard_map/all_to_all | solution.py:315
  120.0 0.7 copy.32
  (44 shorter events, 4.4 us)
Async XLA Ops:
  0.6 31.4 %copy-start.11 = (bf16[24,3072]{1,0:T(8,128)(2,1)S(1)}, bf16[24,3072]{1,0:T(8,128)(2,1)}, u32[]{:S(2)}) copy-start(bf16[24,3072]{1,0:T(8,128)(2,1)} %param.11) | copy-start | bytes 442372
  0.7 31.3 %copy-start.10 = (bf16[24,3072]{1,0:T(8,128)(2,1)S(1)}, bf16[24,3072]{1,0:T(8,128)(2,1)}, u32[]{:S(2)}) copy-start(bf16[24,3072]{1,0:T(8,128)(2,1)} %param.8) | copy-start | bytes 442372
  29.2 26.1 %copy-start.1 = (bf16[32,24,256]{2,1,0:T(8,128)(2,1)}, bf16[32,24,256]{2,1,0:T(8,128)(2,1)S(1)}, u32[]{:S(2)}) copy-start(bf16[32,24,256]{2,1,0:T(8,128)(2,1)S(1)} %all_to_all.20) | copy-start | bytes 1179652
  29.2 2.8 %collective-permute-start = (bf16[768,256]{1,0:T(8,128)(2,1)S(1)}, bf16[768,256]{1,0:T(8,128)(2,1)S(1)}, u32[]{:S(2)}, u32[]{:S(2)}) collective-permute-start(bf16[768,256]{1,0:T(8,128)(2,1)S(1)} %bitcast.50), channel_id=1, source_target_pairs={{0,8},{8,0},{1,9},{9,1},{2,10},{10,2},{3,11},{11,3},{4,12},{12,4},... | collective-permute-start | bytes 1179656 | tf_op jit(solution)/shard_map/ppermute | solution.py:299
  29.2 20.3 %collective-permute-start.3 = (bf16[768,256]{1,0:T(8,128)(2,1)S(1)}, bf16[768,256]{1,0:T(8,128)(2,1)S(1)}, u32[]{:S(2)}, u32[]{:S(2)}) collective-permute-start(bf16[768,256]{1,0:T(8,128)(2,1)S(1)} %bitcast.51), channel_id=1, source_target_pairs={{0,48},{16,0},{32,16},{48,32},{1,49},{17,1},{33,17},{49,33},{2,50}... | collective-permute-start | bytes 1179656 | tf_op jit(solution)/shard_map/ppermute | solution.py:295
  31.9 20.9 %collective-permute-start.1 = (bf16[768,256]{1,0:T(8,128)(2,1)S(1)}, bf16[768,256]{1,0:T(8,128)(2,1)S(1)}, u32[]{:S(2)}, u32[]{:S(2)}) collective-permute-start(bf16[768,256]{1,0:T(8,128)(2,1)S(1)} %bitcast.52), channel_id=1, source_target_pairs={{0,16},{16,32},{32,48},{48,0},{1,17},{17,33},{33,49},{49,1},{2,18}... | collective-permute-start | bytes 1179656 | tf_op jit(solution)/shard_map/ppermute | solution.py:295
  32.0 23.3 %copy-start.4 = (bf16[768,256]{1,0:T(8,128)(2,1)}, bf16[768,256]{1,0:T(8,128)(2,1)S(1)}, u32[]{:S(2)}) copy-start(bf16[768,256]{1,0:T(8,128)(2,1)S(1)} %collective-permute-done.refs_4_) | copy-start | bytes 1179652
  32.0 20.8 %collective-permute-start.2 = (bf16[768,256]{1,0:T(8,128)(2,1)S(1)}, bf16[768,256]{1,0:T(8,128)(2,1)S(1)}, u32[]{:S(2)}, u32[]{:S(2)}) collective-permute-start(bf16[768,256]{1,0:T(8,128)(2,1)S(1)} %bitcast.53), channel_id=1, source_target_pairs={{0,32},{16,48},{32,0},{48,16},{1,33},{17,49},{33,1},{49,17},{2,34}... | collective-permute-start | bytes 1179656 | tf_op jit(solution)/shard_map/ppermute | solution.py:295
  35.2 19.7 %all-to-all-start.1 = ((bf16[32,24,256]{2,1,0:T(8,128)(2,1)}), bf16[32,24,256]{2,1,0:T(8,128)(2,1)S(1)}, u32[]{:S(2)}, u32[]{:S(2)}) async-start(bf16[32,24,256]{2,1,0:T(8,128)(2,1)} %fusion.4), calls=%async_computation.1 | async-start | bytes 786432 | tf_op jit(solution)/shard_map/all_to_all | solution.py:315
  49.4 5.8 %copy-start.5 = (bf16[768,256]{1,0:T(8,128)(2,1)}, bf16[768,256]{1,0:T(8,128)(2,1)S(1)}, u32[]{:S(2)}) copy-start(bf16[768,256]{1,0:T(8,128)(2,1)S(1)} %collective-permute-done.3.refs_3_) | copy-start | bytes 1179652
  49.5 3.9 %collective-permute-start.6 = (bf16[768,256]{1,0:T(8,128)(2,1)S(1)}, bf16[768,256]{1,0:T(8,128)(2,1)S(1)}, u32[]{:S(2)}, u32[]{:S(2)}) collective-permute-start(bf16[768,256]{1,0:T(8,128)(2,1)S(1)} %collective-permute-done.3.refs_3_), channel_id=1, source_target_pairs={{0,8},{8,0},{1,9},{9,1},{2,10},{10,2},{3,11},{11,3},{4,12},{12,4},... | collective-permute-start | bytes 1179656 | tf_op jit(solution)/shard_map/ppermute | solution.py:299
  52.8 2.4 %copy-start.6 = (bf16[768,256]{1,0:T(8,128)(2,1)}, bf16[768,256]{1,0:T(8,128)(2,1)S(1)}, u32[]{:S(2)}) copy-start(bf16[768,256]{1,0:T(8,128)(2,1)S(1)} %collective-permute-done.1.refs_1_) | copy-start | bytes 1179652
  52.8 1.7 %collective-permute-start.4 = (bf16[768,256]{1,0:T(8,128)(2,1)S(1)}, bf16[768,256]{1,0:T(8,128)(2,1)S(1)}, u32[]{:S(2)}, u32[]{:S(2)}) collective-permute-start(bf16[768,256]{1,0:T(8,128)(2,1)S(1)} %collective-permute-done.1.refs_1_), channel_id=1, source_target_pairs={{0,8},{8,0},{1,9},{9,1},{2,10},{10,2},{3,11},{11,3},{4,12},{12,4},... | collective-permute-start | bytes 1179656 | tf_op jit(solution)/shard_map/ppermute | solution.py:299
  52.8 2.4 %copy-start.7 = (bf16[768,256]{1,0:T(8,128)(2,1)}, bf16[768,256]{1,0:T(8,128)(2,1)S(1)}, u32[]{:S(2)}) copy-start(bf16[768,256]{1,0:T(8,128)(2,1)S(1)} %collective-permute-done.2.refs_2_) | copy-start | bytes 1179652
  52.8 2.4 %collective-permute-start.5 = (bf16[768,256]{1,0:T(8,128)(2,1)S(1)}, bf16[768,256]{1,0:T(8,128)(2,1)}, u32[]{:S(2)}, u32[]{:S(2)}) collective-permute-start(bf16[768,256]{1,0:T(8,128)(2,1)S(1)} %collective-permute-done.2.refs_2_), channel_id=1, source_target_pairs={{0,8},{8,0},{1,9},{9,1},{2,10},{10,2},{3,11},{11,3},{4,12},{12,4},... | collective-permute-start | bytes 1179656 | tf_op jit(solution)/shard_map/ppermute | solution.py:299
  53.4 1.9 %copy-start.8 = (bf16[768,256]{1,0:T(8,128)(2,1)}, bf16[768,256]{1,0:T(8,128)(2,1)S(1)}, u32[]{:S(2)}) copy-start(bf16[768,256]{1,0:T(8,128)(2,1)S(1)} %collective-permute-done.6.refs_7_) | copy-start | bytes 1179652
  71.5 3.9 %copy-start.3 = (bf16[3072,256]{1,0:T(8,128)(2,1)S(1)}, bf16[3072,256]{1,0:T(8,128)(2,1)}, u32[]{:S(2)}) copy-start(bf16[3072,256]{1,0:T(8,128)(2,1)} %get-tuple-element.17) | copy-start | bytes 4718596
  71.5 2.6 %collective-permute-start.8 = (bf16[1536,256]{1,0:T(8,128)(2,1)}, bf16[1536,256]{1,0:T(8,128)(2,1)S(1)}, u32[]{:S(2)}, u32[]{:S(2)}) collective-permute-start(bf16[1536,256]{1,0:T(8,128)(2,1)} %get-tuple-element.19), channel_id=1, source_target_pairs={{0,8},{8,0},{1,9},{9,1},{2,10},{10,2},{3,11},{11,3},{4,12},{12,4},... | collective-permute-start | bytes 2359304 | tf_op jit(solution)/shard_map/ppermute | solution.py:299
  71.6 3.8 %collective-permute-start.7 = (bf16[1536,256]{1,0:T(8,128)(2,1)}, bf16[1536,256]{1,0:T(8,128)(2,1)S(1)}, u32[]{:S(2)}, u32[]{:S(2)}) collective-permute-start(bf16[1536,256]{1,0:T(8,128)(2,1)} %get-tuple-element.18), channel_id=1, source_target_pairs={{0,8},{8,0},{1,9},{9,1},{2,10},{10,2},{3,11},{11,3},{4,12},{12,4},... | collective-permute-start | bytes 2359304 | tf_op jit(solution)/shard_map/ppermute | solution.py:299
  76.3 13.8 %collective-permute-start.11 = (bf16[768,256]{1,0:T(8,128)(2,1)}, bf16[768,256]{1,0:T(8,128)(2,1)}, u32[]{:S(2)}, u32[]{:S(2)}) collective-permute-start(bf16[768,256]{1,0:T(8,128)(2,1)} %add_convert_fusion.1), channel_id=1, source_target_pairs={{0,32},{16,48},{32,0},{48,16},{1,33},{17,49},{33,1},{49,17},{2,34}... | collective-permute-start | bytes 1179656 | tf_op jit(solution)/shard_map/ppermute | solution.py:295
  79.3 16.9 %collective-permute-start.10 = (bf16[768,256]{1,0:T(8,128)(2,1)S(1)}, bf16[768,256]{1,0:T(8,128)(2,1)}, u32[]{:S(2)}, u32[]{:S(2)}) collective-permute-start(bf16[768,256]{1,0:T(8,128)(2,1)S(1)} %get-tuple-element.21), channel_id=1, source_target_pairs={{0,48},{16,0},{32,16},{48,32},{1,49},{17,1},{33,17},{49,33},{2,50}... | collective-permute-start | bytes 1179656 | tf_op jit(solution)/shard_map/ppermute | solution.py:295
  80.7 16.9 %collective-permute-start.9 = (bf16[768,256]{1,0:T(8,128)(2,1)S(1)}, bf16[768,256]{1,0:T(8,128)(2,1)}, u32[]{:S(2)}, u32[]{:S(2)}) collective-permute-start(bf16[768,256]{1,0:T(8,128)(2,1)S(1)} %get-tuple-element.22), channel_id=1, source_target_pairs={{0,16},{16,32},{32,48},{48,0},{1,17},{17,33},{33,49},{49,1},{2,18}... | collective-permute-start | bytes 1179656 | tf_op jit(solution)/shard_map/ppermute | solution.py:295
  81.4 18.5 %all-to-all-start.2 = ((bf16[32,24,128]{2,1,0:T(8,128)(2,1)}), bf16[32,24,128]{2,1,0:T(8,128)(2,1)S(1)}, u32[]{:S(2)}, u32[]{:S(2)}) async-start(bf16[32,24,128]{2,1,0:T(8,128)(2,1)} %bitcast.56), calls=%async_computation.2 | async-start | bytes 393216 | tf_op jit(solution)/shard_map/all_to_all | solution.py:315
  99.9 20.1 %all-to-all-start.3 = ((bf16[32,24,256]{2,1,0:T(8,128)(2,1)}), bf16[32,24,256]{2,1,0:T(8,128)(2,1)S(1)}, u32[]{:S(2)}, u32[]{:S(2)}) async-start(bf16[32,24,256]{2,1,0:T(8,128)(2,1)} %bitcast.8), calls=%async_computation.3 | async-start | bytes 786432 | tf_op jit(solution)/shard_map/all_to_all | solution.py:315
  (3 other events, 2.5 us)

commit v4 on v3

--- a/solution.py
+++ b/solution.py
@@ -40,9 +40,9 @@
 
 def attend_kernel(slots, lengths, steps, qd, gain, *refs):
     chunks = refs[0:8]
-    dq_hbm, mine_hbm, near_hbm, far_hbm = refs[8:12]
-    (kv, kt, q_rows, d_rows, q_cols, d_cols, head_gain, spans, weights, d_probs, dkv, dq_cols, dq_rows) = refs[12:25]
-    (tops, weight_sums, product_sums, delta, sources, targets, q_sems, kv_sems, out_sems) = refs[25:]
+    dq_hbm, out_hbm = refs[8], refs[9:13]
+    (kv, kt, q_rows, d_rows, q_cols, d_cols, head_gain, spans, weights, d_probs, dkv, dq_cols, dq_rows) = refs[13:26]
+    (tops, weight_sums, product_sums, delta, sources, targets, q_sems, kv_sems, out_sems) = refs[26:]
     my_x, my_core, my_head = place()
 
     def slot_at(zlo, x, core):
@@ -89,6 +89,10 @@
     def end_of(position):
         return sum(jnp.where(starts[s] <= position, lengths[s], 0) for s in range(SEGMENTS))
 
+    def gain_at(position):
+        span = sum((ends[s] <= position).astype(jnp.int32) for s in range(SEGMENTS))
+        return head_gain[pl.ds(steps[span], 1), :]
+
     def positions(shape, dimension):
         index = lax.broadcasted_iota(jnp.int32, shape, dimension)
         base = jnp.where(index < BLK, ordered[0] * BLK, ordered[1] * BLK - BLK)
@@ -144,12 +148,12 @@
         d_rows[block(ranks[b]), :] = qd[b * BLK : (b + 1) * BLK, HD:]
     head_gain[...] = gain[:, pl.ds(pl.multiple_of(my_head * HD, HD), HD)]
     q_cols[0:HD, :] = q_rows[...].T
-    row_positions = positions((QROWS, 1), 0)
-    row_gain = jnp.zeros((QROWS, HD), jnp.float32)
-    for s in range(SEGMENTS):
-        inside = (starts[s] <= row_positions) & (row_positions < ends[s])
-        row_gain = jnp.where(inside, head_gain[pl.ds(steps[s], 1), :], row_gain)
-    d_rows[...] = (d_rows[...].astype(jnp.float32) * row_gain).astype(jnp.bfloat16)
+    for r in range(ZLO):
+        at = slice(r * BLK, (r + 1) * BLK)
+        first, last = ordered[r] * BLK, (ordered[r] + 1) * BLK - 1
+        early = lax.broadcasted_iota(jnp.int32, (BLK, 1), 0) + first < end_of(first)
+        row_gain = jnp.where(early, gain_at(first), gain_at(last))
+        d_rows[at, :] = (d_rows[at, :].astype(jnp.float32) * row_gain).astype(jnp.bfloat16)
     d_cols[...] = d_rows[...].T
 
     def leave(t):
@@ -157,23 +161,13 @@
             slot = t * (TK // BLK) + i
             target = targets[slot]
 
-            @pl.when(target < X * ZLO)
-            def _():
-                pltpu.make_async_copy(
-                    dkv.at[block(slot)], mine_hbm.at[block(target)], out_sems.at[slot]
-                ).start()
-
-            @pl.when((target >= X * ZLO) & (target < (X + 2) * ZLO))
-            def _():
-                pltpu.make_async_copy(
-                    dkv.at[block(slot)], near_hbm.at[block(target - X * ZLO)], out_sems.at[slot]
-                ).start()
-
-            @pl.when(target >= (X + 2) * ZLO)
-            def _():
-                pltpu.make_async_copy(
-                    dkv.at[block(slot)], far_hbm.at[block(target - (X + 2) * ZLO)], out_sems.at[slot]
-                ).start()
+            for i in range(4):
+
+                @pl.when((target >= i * 2 * ZLO) & (target < (i + 1) * 2 * ZLO))
+                def _():
+                    pltpu.make_async_copy(
+                        dkv.at[block(slot)], out_hbm[i].at[block(target - i * 2 * ZLO)], out_sems.at[slot]
+                    ).start()
 
     def total(array):
         return jnp.sum(jnp.sum(array.reshape(-1, 8, array.shape[1]), axis=0), axis=0, keepdims=True)
@@ -243,7 +237,7 @@
     for copy in out_copies:
         copy.start()
     for slot in range(TOKENS // BLK):
-        pltpu.make_async_copy(dkv.at[block(slot)], mine_hbm.at[block(0)], out_sems.at[slot]).wait()
+        pltpu.make_async_copy(dkv.at[block(slot)], out_hbm[0].at[block(0)], out_sems.at[slot]).wait()
     for copy in out_copies:
         copy.wait()
 
@@ -254,10 +248,7 @@
     low = jnp.bfloat16
     outs = [
         jax.ShapeDtypeStruct((QROWS, HD), low),
-        jax.ShapeDtypeStruct((X * QROWS, 2 * HD), low),
-        jax.ShapeDtypeStruct((2 * QROWS, 2 * HD), low),
-        jax.ShapeDtypeStruct((2 * QROWS, 2 * HD), low),
-    ]
+    ] + [jax.ShapeDtypeStruct((2 * QROWS, 2 * HD), low)] * 4
     return pl.pallas_call(
         attend_kernel,
         out_shape=outs,
@@ -324,15 +315,18 @@
     kv = exchange(by_head(keys, values)).reshape(QROWS, 2 * HD)
     beside = other_core(kv)
     near = {s: x_shift(kv, s) for s in (1, 3)}
-    later, queries, d_out, beside = lax.optimization_barrier((kv, queries, d_out, beside))
+    queries, d_out, beside = lax.optimization_barrier((queries, d_out, beside))
+    later, qd = lax.optimization_barrier((kv, by_head(queries, d_out)))
     own = [kv, near[1], x_shift(later, 2), near[3]]
-    qd = exchange(by_head(queries, d_out)).reshape(QROWS, 2 * HD)
+    qd = exchange(qd).reshape(QROWS, 2 * HD)
     chunks = own + [beside] + [other_core(c) for c in own[1:]]
-    dq, mine, other_near, other_far = attend(slots, lengths, steps, qd, gain, chunks)
-    received_near, received_far = other_core(other_near), other_core(other_far)
+    dq, near, far, other_near, other_far = attend(slots, lengths, steps, qd, gain, chunks)
+    received_near = other_core(other_near)
+    other_far, received_near = lax.optimization_barrier((other_far, received_near))
+    received_far = other_core(other_far)
 
     def pair(shift, received):
-        return part(mine, shift).astype(jnp.float32) + part(received, shift).astype(jnp.float32)
+        return part(near if shift in SENT[:2] else far, shift).astype(jnp.float32) + part(received, shift).astype(jnp.float32)
 
     pairs = [pair(s, received_near).astype(jnp.bfloat16) for s in SENT[:2]]
     arrived = [x_shift(p, s) for p, s in zip(pairs, SENT)]

time: 123 us -> 122 us (level)
  starting transfers between devices: 24.3 us -> 26.4 us
  Pallas kernels: 15.8 us -> 14 us
  waiting for transfers between devices: 44.3 us -> 43 us
    pallas_call x1, Pallas kernels: 15.8 us -> 14 us  [attend(): pl.pallas_call(attend_kernel, out_shape=outs, in_specs=[smem] * 3 + [pl.B...]
    all_to_all x3, starting transfers between devices: 13 us -> 14.7 us  [exchange(): lax.all_to_all(array, COLUMNS, split_axis=0, concat_axis=0, tiled=True)]
  transfers between devices with their start and end apart: 15 -> 15, of which waited for: 10 -> 9; matrix products, arithmetic and copies ran while one was open for 4% -> 5% of each run, Pallas kernels for 0% -> 0%
where the time goes in v4:
time: 122 us; the launch traced here: 121 us
  waiting for transfers between devices  43 us (35%)
  blocking collectives  26.7 us (22%)
  starting transfers between devices  26.4 us (22%)
  Pallas kernels  14 us (11%)
  other arithmetic  5.06 us (4%)
  local copies, waits for them, and re-layouts  4.81 us (4%)
    all_to_all x1, blocking collectives, exchange(): lax.all_to_all(array, COLUMNS, split_axis=0, concat_axis=0, tiled=True)  26.7 us
    ppermute x6, waiting for transfers between devices, x_shift(): return lax.ppermute(array, 'x', [(i, (i + shift) % X) for i in range(X)])  25 us
    all_to_all x3, starting transfers between devices, exchange(): lax.all_to_all(array, COLUMNS, split_axis=0, concat_axis=0, tiled=True)  14.7 us
    all_to_all x3, waiting for transfers between devices, exchange(): lax.all_to_all(array, COLUMNS, split_axis=0, concat_axis=0, tiled=True)  14.5 us
    pallas_call x1, Pallas kernels, attend(): pl.pallas_call(attend_kernel, out_shape=outs, in_specs=[smem] * 3 + [pl.B...  14 us
    ppermute x6, starting transfers between devices, x_shift(): return lax.ppermute(array, 'x', [(i, (i + shift) % X) for i in range(X)])  10.2 us
    ppermute x6, waiting for transfers between devices, other_core(): return lax.ppermute(array, 'core', [(0, 1), (1, 0)])  3.47 us
  transfers between devices with their start and end apart: 15, of which 9 were waited for; matrix products, arithmetic and copies ran while one was open for 5% of the time, Pallas kernels for 0%

profile of v4, /device:TPU:32, one launch (start us, length us, event | category | flops | bytes accessed | tf_op | source)
XLA Modules:
  0.0 120.8 jit_solution(4023416382007037391)
XLA Ops:
  0.6 0.9 copy-done
  1.5 1.0 bitcast_bitcast_fusion.2
  2.6 26.7 %all_to_all.20 = bf16[32,24,256]{2,1,0:T(8,128)(2,1)S(1)} all-to-all(bf16[32,24,256]{2,1,0:T(8,128)(2,1)S(1)} %fusion.4), channel_id=1, replica_groups=mesh['zlo'=4,'x'=4,'core'=2,'zhi'=2,'y'=4] {'zlo','zhi','y'}, dimensions={0} | all-to-all | bytes 786432 | tf_op jit(solution)/shard_map/all_to_all | solution.py:306
  29.3 2.8 %collective-permute-start.3 = (bf16[768,256]{1,0:T(8,128)(2,1)S(1)}, bf16[768,256]{1,0:T(8,128)(2,1)S(1)}, u32[]{:S(2)}, u32[]{:S(2)}) collective-permute-start(bf16[768,256]{1,0:T(8,128)(2,1)S(1)} %bitcast.51), channel_id=1, source_target_pairs={{0,48},{16,0},{32,16},{48,32},{1,49},{17,1},{33,17},{49,33},{2,50}... | collective-permute-start | bytes 1179656 | tf_op jit(solution)/shard_map/ppermute | solution.py:286
  32.2 0.8 fusion.5
  33.0 2.3 %collective-permute-start.2 = (bf16[768,256]{1,0:T(8,128)(2,1)S(1)}, bf16[768,256]{1,0:T(8,128)(2,1)S(1)}, u32[]{:S(2)}, u32[]{:S(2)}) collective-permute-start(bf16[768,256]{1,0:T(8,128)(2,1)S(1)} %bitcast.53), channel_id=1, source_target_pairs={{0,32},{16,48},{32,0},{48,16},{1,33},{17,49},{33,1},{49,17},{2,34}... | collective-permute-start | bytes 1179656 | tf_op jit(solution)/shard_map/ppermute | solution.py:286
  35.3 4.3 %all-to-all-start.1 = ((bf16[32,24,256]{2,1,0:T(8,128)(2,1)}), bf16[32,24,256]{2,1,0:T(8,128)(2,1)S(1)}, u32[]{:S(2)}, u32[]{:S(2)}) async-start(bf16[32,24,256]{2,1,0:T(8,128)(2,1)} %fusion.5), calls=%async_computation.1 | async-start | bytes 786432 | tf_op jit(solution)/shard_map/all_to_all | solution.py:306
  39.6 9.9 %collective-permute-done.3.refs_3_ = bf16[768,256]{1,0:T(8,128)(2,1)S(1)} collective-permute-done((bf16[768,256]{1,0:T(8,128)(2,1)S(1)}, bf16[768,256]{1,0:T(8,128)(2,1)S(1)}, u32[]{:S(2)}, u32[]{:S(2)}) %collective-permute-start.3) | collective-permute-done | bytes 393248 | tf_op jit(solution)/shard_map/ppermute | solution.py:286
  49.5 3.4 %collective-permute-done.1.refs_1_ = bf16[768,256]{1,0:T(8,128)(2,1)S(1)} collective-permute-done((bf16[768,256]{1,0:T(8,128)(2,1)S(1)}, bf16[768,256]{1,0:T(8,128)(2,1)S(1)}, u32[]{:S(2)}, u32[]{:S(2)}) %collective-permute-start.1) | collective-permute-done | bytes 393248 | tf_op jit(solution)/shard_map/ppermute | solution.py:286
  53.4 1.2 collective-permute-done.4.refs_5_
  56.0 14.0 %shard_map.103 = (bf16[768,128]{1,0:T(8,128)(2,1)}, bf16[1536,256]{1,0:T(8,128)(2,1)}, bf16[1536,256]{1,0:T(8,128)(2,1)}, bf16[1536,256]{1,0:T(8,128)(2,1)}, bf16[1536,256]{1,0:T(8,128)(2,1)}) custom-call(s32[32]{0:T(128)} %slots.1, s32[8]{0:T(128)} %lengths.1, s32[8]{0:T(128)} %steps.1, bf16[768,256]{1,0:T(8,128)(2,1)} %bitcast.55, f32[16,3072]{1,0:T(8,128)} %gain.1, ...), custom_call_target="tpu_custom_call" | custom-call | tf_op jit(solution)/shard_map/pallas_call | solution.py:252
  70.6 2.1 %collective-permute-done.7 = bf16[1536,256]{1,0:T(8,128)(2,1)S(1)} collective-permute-done((bf16[1536,256]{1,0:T(8,128)(2,1)}, bf16[1536,256]{1,0:T(8,128)(2,1)S(1)}, u32[]{:S(2)}, u32[]{:S(2)}) %collective-permute-start.7) | collective-permute-done | bytes 786464 | tf_op jit(solution)/shard_map/ppermute | solution.py:290
  73.1 1.4 %add_convert_fusion.2 = (bf16[768,256]{1,0:T(8,128)(2,1)S(1)}, bf16[768,256]{1,0:T(8,128)(2,1)S(1)}) fusion(bf16[1536,256]{1,0:T(8,128)(2,1)S(1)} %collective-permute-done.7, bf16[1536,256]{1,0:T(8,128)(2,1)} %get-tuple-element.26), kind=kLoop, calls=%fused_computation.7 | loop fusion | flops 1572864 | bytes 2359296 | tf_op jit(solution)/shard_map/convert_element_type | solution.py:331
  74.4 2.5 %collective-permute-start.10 = (bf16[768,256]{1,0:T(8,128)(2,1)S(1)}, bf16[768,256]{1,0:T(8,128)(2,1)S(1)}, u32[]{:S(2)}, u32[]{:S(2)}) collective-permute-start(bf16[768,256]{1,0:T(8,128)(2,1)S(1)} %get-tuple-element.29), channel_id=1, source_target_pairs={{0,48},{16,0},{32,16},{48,32},{1,49},{17,1},{33,17},{49,33},{2,50}... | collective-permute-start | bytes 1179656 | tf_op jit(solution)/shard_map/ppermute | solution.py:286
  77.6 0.9 add_convert_fusion.1
  78.4 2.0 %collective-permute-start.11 = (bf16[768,256]{1,0:T(8,128)(2,1)}, bf16[768,256]{1,0:T(8,128)(2,1)}, u32[]{:S(2)}, u32[]{:S(2)}) collective-permute-start(bf16[768,256]{1,0:T(8,128)(2,1)} %add_convert_fusion.1), channel_id=1, source_target_pairs={{0,32},{16,48},{32,0},{48,16},{1,33},{17,49},{33,1},{49,17},{2,34}... | collective-permute-start | bytes 1179656 | tf_op jit(solution)/shard_map/ppermute | solution.py:286
  80.4 5.3 %all-to-all-start.2 = ((bf16[32,24,128]{2,1,0:T(8,128)(2,1)}), bf16[32,24,128]{2,1,0:T(8,128)(2,1)S(1)}, u32[]{:S(2)}, u32[]{:S(2)}) async-start(bf16[32,24,128]{2,1,0:T(8,128)(2,1)} %bitcast.56), calls=%async_computation.2 | async-start | bytes 393216 | tf_op jit(solution)/shard_map/all_to_all | solution.py:306
  85.7 1.6 %collective-permute-done.10 = bf16[768,256]{1,0:T(8,128)(2,1)S(1)} collective-permute-done((bf16[768,256]{1,0:T(8,128)(2,1)S(1)}, bf16[768,256]{1,0:T(8,128)(2,1)S(1)}, u32[]{:S(2)}, u32[]{:S(2)}) %collective-permute-start.10) | collective-permute-done | bytes 393248 | tf_op jit(solution)/shard_map/ppermute | solution.py:286
  87.4 10.1 %collective-permute-done.9 = bf16[768,256]{1,0:T(8,128)(2,1)S(1)} collective-permute-done((bf16[768,256]{1,0:T(8,128)(2,1)S(1)}, bf16[768,256]{1,0:T(8,128)(2,1)S(1)}, u32[]{:S(2)}, u32[]{:S(2)}) %collective-permute-start.9) | collective-permute-done | bytes 393248 | tf_op jit(solution)/shard_map/ppermute | solution.py:286
  97.5 2.0 %add_convert_fusion = bf16[768,256]{1,0:T(8,128)(2,1)} fusion(bf16[768,256]{1,0:T(8,128)(2,1)} %collective-permute-done.11, bf16[768,256]{1,0:T(8,128)(2,1)S(1)} %collective-permute-done.10, bf16[768,256]{1,0:T(8,128)(2,1)S(1)} %collective-permute-done.9, bf16[1536,256]{1,0:T(8,128)(2,1)S(1)} %collective-permute-done.8, bf16[1536,256]{1,0:T(8,128)(2,1)S(1)} %copy-done.3), kind=kLoop, calls=%fused_computation.5 | loop fusion | flops 1966080 | bytes 2359296 | tf_op jit(solution)/shard_map/convert_element_type | solution.py:338
  99.5 5.1 %all-to-all-start.3 = ((bf16[32,24,256]{2,1,0:T(8,128)(2,1)}), bf16[32,24,256]{2,1,0:T(8,128)(2,1)S(1)}, u32[]{:S(2)}, u32[]{:S(2)}) async-start(bf16[32,24,256]{2,1,0:T(8,128)(2,1)} %bitcast.8), calls=%async_computation.3 | async-start | bytes 786432 | tf_op jit(solution)/shard_map/all_to_all | solution.py:306
  105.2 14.1 %all-to-all-done.3 = bf16[32,24,256]{2,1,0:T(8,128)(2,1)S(1)} async-done(((bf16[32,24,256]{2,1,0:T(8,128)(2,1)}), bf16[32,24,256]{2,1,0:T(8,128)(2,1)S(1)}, u32[]{:S(2)}, u32[]{:S(2)}) %all-to-all-start.3) | async-done | bytes 393248 | tf_op jit(solution)/shard_map/all_to_all | solution.py:306
  119.4 0.7 copy.32
  120.1 0.7 copy.33
  (46 shorter events, 4.3 us)
Async XLA Ops:
  0.6 0.9 copy-start
  2.6 29.5 %copy-start.11 = (bf16[24,3072]{1,0:T(8,128)(2,1)S(1)}, bf16[24,3072]{1,0:T(8,128)(2,1)}, u32[]{:S(2)}) copy-start(bf16[24,3072]{1,0:T(8,128)(2,1)} %param.8) | copy-start | bytes 442372
  29.3 3.7 %copy-start.1 = (bf16[32,24,256]{2,1,0:T(8,128)(2,1)}, bf16[32,24,256]{2,1,0:T(8,128)(2,1)S(1)}, u32[]{:S(2)}) copy-start(bf16[32,24,256]{2,1,0:T(8,128)(2,1)S(1)} %all_to_all.20) | copy-start | bytes 1179652
  29.3 2.9 %copy-start.12 = (bf16[24,3072]{1,0:T(8,128)(2,1)S(1)}, bf16[24,3072]{1,0:T(8,128)(2,1)}, u32[]{:S(2)}) copy-start(bf16[24,3072]{1,0:T(8,128)(2,1)} %param.11) | copy-start | bytes 442372
  29.3 2.8 %collective-permute-start = (bf16[768,256]{1,0:T(8,128)(2,1)S(1)}, bf16[768,256]{1,0:T(8,128)(2,1)S(1)}, u32[]{:S(2)}, u32[]{:S(2)}) collective-permute-start(bf16[768,256]{1,0:T(8,128)(2,1)S(1)} %bitcast.50), channel_id=1, source_target_pairs={{0,8},{8,0},{1,9},{9,1},{2,10},{10,2},{3,11},{11,3},{4,12},{12,4},... | collective-permute-start | bytes 1179656 | tf_op jit(solution)/shard_map/ppermute | solution.py:290
  29.3 20.3 %collective-permute-start.3 = (bf16[768,256]{1,0:T(8,128)(2,1)S(1)}, bf16[768,256]{1,0:T(8,128)(2,1)S(1)}, u32[]{:S(2)}, u32[]{:S(2)}) collective-permute-start(bf16[768,256]{1,0:T(8,128)(2,1)S(1)} %bitcast.51), channel_id=1, source_target_pairs={{0,48},{16,0},{32,16},{48,32},{1,49},{17,1},{33,17},{49,33},{2,50}... | collective-permute-start | bytes 1179656 | tf_op jit(solution)/shard_map/ppermute | solution.py:286
  32.1 20.8 %collective-permute-start.1 = (bf16[768,256]{1,0:T(8,128)(2,1)S(1)}, bf16[768,256]{1,0:T(8,128)(2,1)S(1)}, u32[]{:S(2)}, u32[]{:S(2)}) collective-permute-start(bf16[768,256]{1,0:T(8,128)(2,1)S(1)} %bitcast.52), channel_id=1, source_target_pairs={{0,16},{16,32},{32,48},{48,0},{1,17},{17,33},{33,49},{49,1},{2,18}... | collective-permute-start | bytes 1179656 | tf_op jit(solution)/shard_map/ppermute | solution.py:286
  33.0 19.9 %collective-permute-start.2 = (bf16[768,256]{1,0:T(8,128)(2,1)S(1)}, bf16[768,256]{1,0:T(8,128)(2,1)S(1)}, u32[]{:S(2)}, u32[]{:S(2)}) collective-permute-start(bf16[768,256]{1,0:T(8,128)(2,1)S(1)} %bitcast.53), channel_id=1, source_target_pairs={{0,32},{16,48},{32,0},{48,16},{1,33},{17,49},{33,1},{49,17},{2,34}... | collective-permute-start | bytes 1179656 | tf_op jit(solution)/shard_map/ppermute | solution.py:286
  35.3 19.8 %all-to-all-start.1 = ((bf16[32,24,256]{2,1,0:T(8,128)(2,1)}), bf16[32,24,256]{2,1,0:T(8,128)(2,1)S(1)}, u32[]{:S(2)}, u32[]{:S(2)}) async-start(bf16[32,24,256]{2,1,0:T(8,128)(2,1)} %fusion.5), calls=%async_computation.1 | async-start | bytes 786432 | tf_op jit(solution)/shard_map/all_to_all | solution.py:306
  49.5 5.7 %copy-start.5 = (bf16[768,256]{1,0:T(8,128)(2,1)}, bf16[768,256]{1,0:T(8,128)(2,1)S(1)}, u32[]{:S(2)}) copy-start(bf16[768,256]{1,0:T(8,128)(2,1)S(1)} %collective-permute-done.3.refs_3_) | copy-start | bytes 1179652
  49.5 3.9 %collective-permute-start.6 = (bf16[768,256]{1,0:T(8,128)(2,1)S(1)}, bf16[768,256]{1,0:T(8,128)(2,1)S(1)}, u32[]{:S(2)}, u32[]{:S(2)}) collective-permute-start(bf16[768,256]{1,0:T(8,128)(2,1)S(1)} %collective-permute-done.3.refs_3_), channel_id=1, source_target_pairs={{0,8},{8,0},{1,9},{9,1},{2,10},{10,2},{3,11},{11,3},{4,12},{12,4},... | collective-permute-start | bytes 1179656 | tf_op jit(solution)/shard_map/ppermute | solution.py:290
  52.9 2.3 %copy-start.6 = (bf16[768,256]{1,0:T(8,128)(2,1)}, bf16[768,256]{1,0:T(8,128)(2,1)S(1)}, u32[]{:S(2)}) copy-start(bf16[768,256]{1,0:T(8,128)(2,1)S(1)} %collective-permute-done.1.refs_1_) | copy-start | bytes 1179652
  52.9 1.7 %collective-permute-start.4 = (bf16[768,256]{1,0:T(8,128)(2,1)S(1)}, bf16[768,256]{1,0:T(8,128)(2,1)S(1)}, u32[]{:S(2)}, u32[]{:S(2)}) collective-permute-start(bf16[768,256]{1,0:T(8,128)(2,1)S(1)} %collective-permute-done.1.refs_1_), channel_id=1, source_target_pairs={{0,8},{8,0},{1,9},{9,1},{2,10},{10,2},{3,11},{11,3},{4,12},{12,4},... | collective-permute-start | bytes 1179656 | tf_op jit(solution)/shard_map/ppermute | solution.py:290
  52.9 2.3 %copy-start.7 = (bf16[768,256]{1,0:T(8,128)(2,1)}, bf16[768,256]{1,0:T(8,128)(2,1)S(1)}, u32[]{:S(2)}) copy-start(bf16[768,256]{1,0:T(8,128)(2,1)S(1)} %collective-permute-done.2.refs_2_) | copy-start | bytes 1179652
  52.9 2.3 %collective-permute-start.5 = (bf16[768,256]{1,0:T(8,128)(2,1)S(1)}, bf16[768,256]{1,0:T(8,128)(2,1)S(1)}, u32[]{:S(2)}, u32[]{:S(2)}) collective-permute-start(bf16[768,256]{1,0:T(8,128)(2,1)S(1)} %collective-permute-done.2.refs_2_), channel_id=1, source_target_pairs={{0,8},{8,0},{1,9},{9,1},{2,10},{10,2},{3,11},{11,3},{4,12},{12,4},... | collective-permute-start | bytes 1179656 | tf_op jit(solution)/shard_map/ppermute | solution.py:290
  53.4 1.8 %copy-start.8 = (bf16[768,256]{1,0:T(8,128)(2,1)}, bf16[768,256]{1,0:T(8,128)(2,1)S(1)}, u32[]{:S(2)}) copy-start(bf16[768,256]{1,0:T(8,128)(2,1)S(1)} %collective-permute-done.6.refs_7_) | copy-start | bytes 1179652
  69.9 2.8 %collective-permute-start.7 = (bf16[1536,256]{1,0:T(8,128)(2,1)}, bf16[1536,256]{1,0:T(8,128)(2,1)S(1)}, u32[]{:S(2)}, u32[]{:S(2)}) collective-permute-start(bf16[1536,256]{1,0:T(8,128)(2,1)} %get-tuple-element.24), channel_id=1, source_target_pairs={{0,8},{8,0},{1,9},{9,1},{2,10},{10,2},{3,11},{11,3},{4,12},{12,4},... | collective-permute-start | bytes 2359304 | tf_op jit(solution)/shard_map/ppermute | solution.py:290
  72.7 4.9 %collective-permute-start.8 = (bf16[1536,256]{1,0:T(8,128)(2,1)}, bf16[1536,256]{1,0:T(8,128)(2,1)S(1)}, u32[]{:S(2)}, u32[]{:S(2)}) collective-permute-start(bf16[1536,256]{1,0:T(8,128)(2,1)} %get-tuple-element.25), channel_id=1, source_target_pairs={{0,8},{8,0},{1,9},{9,1},{2,10},{10,2},{3,11},{11,3},{4,12},{12,4},... | collective-permute-start | bytes 2359304 | tf_op jit(solution)/shard_map/ppermute | solution.py:290
  73.1 4.5 %copy-start.3 = (bf16[1536,256]{1,0:T(8,128)(2,1)S(1)}, bf16[1536,256]{1,0:T(8,128)(2,1)}, u32[]{:S(2)}) copy-start(bf16[1536,256]{1,0:T(8,128)(2,1)} %get-tuple-element.22) | copy-start | bytes 2359300
  74.4 12.9 %collective-permute-start.10 = (bf16[768,256]{1,0:T(8,128)(2,1)S(1)}, bf16[768,256]{1,0:T(8,128)(2,1)S(1)}, u32[]{:S(2)}, u32[]{:S(2)}) collective-permute-start(bf16[768,256]{1,0:T(8,128)(2,1)S(1)} %get-tuple-element.29), channel_id=1, source_target_pairs={{0,48},{16,0},{32,16},{48,32},{1,49},{17,1},{33,17},{49,33},{2,50}... | collective-permute-start | bytes 1179656 | tf_op jit(solution)/shard_map/ppermute | solution.py:286
  77.0 20.5 %collective-permute-start.9 = (bf16[768,256]{1,0:T(8,128)(2,1)S(1)}, bf16[768,256]{1,0:T(8,128)(2,1)S(1)}, u32[]{:S(2)}, u32[]{:S(2)}) collective-permute-start(bf16[768,256]{1,0:T(8,128)(2,1)S(1)} %get-tuple-element.30), channel_id=1, source_target_pairs={{0,16},{16,32},{32,48},{48,0},{1,17},{17,33},{33,49},{49,1},{2,18}... | collective-permute-start | bytes 1179656 | tf_op jit(solution)/shard_map/ppermute | solution.py:286
  78.4 19.1 %collective-permute-start.11 = (bf16[768,256]{1,0:T(8,128)(2,1)}, bf16[768,256]{1,0:T(8,128)(2,1)}, u32[]{:S(2)}, u32[]{:S(2)}) collective-permute-start(bf16[768,256]{1,0:T(8,128)(2,1)} %add_convert_fusion.1), channel_id=1, source_target_pairs={{0,32},{16,48},{32,0},{48,16},{1,33},{17,49},{33,1},{49,17},{2,34}... | collective-permute-start | bytes 1179656 | tf_op jit(solution)/shard_map/ppermute | solution.py:286
  80.4 19.1 %all-to-all-start.2 = ((bf16[32,24,128]{2,1,0:T(8,128)(2,1)}), bf16[32,24,128]{2,1,0:T(8,128)(2,1)S(1)}, u32[]{:S(2)}, u32[]{:S(2)}) async-start(bf16[32,24,128]{2,1,0:T(8,128)(2,1)} %bitcast.56), calls=%async_computation.2 | async-start | bytes 393216 | tf_op jit(solution)/shard_map/all_to_all | solution.py:306
  99.5 19.9 %all-to-all-start.3 = ((bf16[32,24,256]{2,1,0:T(8,128)(2,1)}), bf16[32,24,256]{2,1,0:T(8,128)(2,1)S(1)}, u32[]{:S(2)}, u32[]{:S(2)}) async-start(bf16[32,24,256]{2,1,0:T(8,128)(2,1)} %bitcast.8), calls=%async_computation.3 | async-start | bytes 786432 | tf_op jit(solution)/shard_map/all_to_all | solution.py:306
  (4 other events, 3.2 us)
